TPU v7x, 512 devices: a whole 4x4x16 slice. The times are simulated.
512 devices in a mesh: gx: 64 (over z, y), gy: 8 (over x, core).
Axes of the slice: x: 4, y: 4, z: 16, core: 2. Of those that a mesh axis runs over, the one named last changes fastest.
Arguments:
- tensor: bfloat16 [4096, 64, 4096], P('gx', None, 'gy'), may hold values from -104 to 104
- factor_b: bfloat16 [4096, 256], P('gy'), may hold values from -0.09375 to 0.09375
- factor_c: bfloat16 [64, 256], replicated, may hold values from -0.75 to 0.75
Outputs:
- a_hat: float32 [4096, 256], P('gx')
- b_hat: float32 [4096, 256], P('gy')
All inputs are finite; a program needn't handle non-finite values.
Results may differ from a plain program's by a relative error of at most 0.0019.
The roundings to bfloat16 on the way count: a program that leaves them out, or rounds other values in their place, can miss the bound.
Values sent between devices are 32-bit elements; how exact they have to be, the bound alone decides.
No kernel may reach another device: no remote copies, remote signals or barrier semaphores. Data moves between devices by JAX's collectives and lax.ppermute only.
A program may use at most 64 MiB of HBM per device.

v0:
```python
import jax
import jax.numpy as jnp
from jax import lax
from jax.sharding import PartitionSpec as P

EPSILON = 1e-06


def lower_inverse(symmetric):
    order = symmetric.shape[0]
    if order == 1:
        return 1.0 / jnp.sqrt(symmetric)
    half = order // 2
    w_top = lower_inverse(symmetric[:half, :half])
    l_low = jnp.dot(symmetric[half:, :half], w_top.T, precision=lax.Precision.HIGHEST)
    schur = symmetric[half:, half:] - jnp.dot(l_low, l_low.T, precision=lax.Precision.HIGHEST)
    w_bottom = lower_inverse(schur)
    w_middle = -jnp.dot(
        w_bottom,
        jnp.dot(l_low, w_top, precision=lax.Precision.HIGHEST),
        precision=lax.Precision.HIGHEST,
    )
    upper_band = jnp.concatenate([w_top, jnp.zeros((half, order - half), symmetric.dtype)], axis=1)
    lower_band = jnp.concatenate([w_middle, w_bottom], axis=1)
    return jnp.concatenate([upper_band, lower_band], axis=0)


def solve_rows(gram_matrix, right_rows):
    inverse_factor = lower_inverse(gram_matrix)
    halfway = jnp.dot(right_rows, inverse_factor.T, precision=lax.Precision.HIGHEST)
    return jnp.dot(halfway, inverse_factor, precision=lax.Precision.HIGHEST)


def local(tensor, factor_b, factor_c):
    x_rows, time_len, y_rows = tensor.shape
    rank_width = factor_b.shape[1]
    c_wide = factor_c.astype(jnp.float32)
    c_gram = jnp.dot(factor_c.T, factor_c, preferred_element_type=jnp.float32)
    local_gram = jnp.dot(factor_b.T, factor_b, preferred_element_type=jnp.float32)
    unfolded = tensor.reshape(x_rows * time_len, y_rows)
    contracted = jnp.dot(unfolded, factor_b, preferred_element_type=jnp.float32).reshape(
        x_rows, time_len, rank_width
    )
    first_part = jnp.sum(contracted * c_wide[None], axis=1)
    b_gram, m_first = lax.psum((local_gram, first_part), "gy")
    a_hat = solve_rows(b_gram * c_gram, m_first)
    col_squares = lax.psum(jnp.sum(a_hat * a_hat, axis=0), "gx")
    a_unit = a_hat / jnp.sqrt(col_squares + EPSILON)
    a_gram = lax.psum(jnp.dot(a_unit.T, a_unit, precision=lax.Precision.HIGHEST), "gx")
    khatri_rao = (
        (a_unit[:, None, :] * c_wide[None])
        .astype(jnp.bfloat16)
        .reshape(x_rows * time_len, rank_width)
    )
    second_gram = a_gram * c_gram
    product = lax.dot_general(
        unfolded, khatri_rao, (((0,), (0,)), ((), ())), preferred_element_type=jnp.float32
    )
    b_hat = solve_rows(second_gram, lax.psum(product, "gx"))
    return (a_hat, b_hat)


def solution(mesh):
    placed = (P("gx", None, "gy"), P("gy", None), P())
    return jax.shard_map(
        local, mesh=mesh, in_specs=placed, out_specs=(P("gx", None), P("gy", None)), check_vma=False
    )
```

profile of v0, /device:TPU:4, one launch (start us, length us, event | category | flops | bytes accessed | tf_op | source)
XLA Modules:
  0.0 1344.2 jit_solution(5764909663547460391)
XLA Ops:
  7.2 0.8 convert_element_type.6
  8.1 1.0 fusion.4276
  9.1 4.1 multiply_reduce_fusion
  13.3 76.3 %all-reduce.261.cloned.1.call-done = (f32[64,256]{1,0:T(8,128)}, f32[256,256]{1,0:T(8,128)}) async-done(((f32[64,256]{1,0:T(8,128)}, f32[256,256]{1,0:T(8,128)}), (f32[64,256]{1,0:T(8,128)}, f32[256,256]{1,0:T(8,128)})) %all-reduce.261.cloned.1.call-update) | async-done | bytes 327696 | tf_op jit(solution)/shard_map/psum | solution.py:45
  89.5 1.2 fusion.4275
  506.0 144.3 %psum.37 = f32[256]{0:T(256)S(1)} all-reduce(f32[256]{0:T(256)S(1)} %get-tuple-element.776), channel_id=1, replica_groups=mesh['gx'=64,'gy'=8] {'gx'}, use_global_device_ids=true, to_apply=%region_4.0 | all-reduce | flops 256 | bytes 2048 | tf_op jit(solution)/shard_map/psum | solution.py:47
  650.3 1.1 fusion.4405
  651.5 4.3 fusion.3
  655.8 266.0 %all-reduce.259.cloned.1.call-done = (f32[512,256]{0,1:T(8,128)}, f32[256,256]{1,0:T(8,128)}) async-done(((f32[512,256]{0,1:T(8,128)}, f32[256,256]{1,0:T(8,128)}), (f32[512,256]{0,1:T(8,128)}, f32[256,256]{1,0:T(8,128)})) %all-reduce.259.cloned.1.call-update) | async-done | bytes 786448 | tf_op jit(solution)/shard_map/psum | solution.py:59
  921.7 1.0 mul.34
  951.1 0.6 fusion.4206
  963.7 0.6 fusion.4204
  1015.0 0.6 fusion.4196
  1028.4 0.6 fusion.4194
  1053.9 0.6 fusion.4190
  1066.5 0.6 fusion.4188
  1183.1 0.6 fusion.4170
  1195.7 0.6 fusion.4168
  1208.6 0.6 fusion.4166
  1234.6 0.6 fusion.4162
  1247.3 0.6 fusion.4160
  1260.1 0.6 fusion.4158
  1334.4 1.0 fusion.4017
  1335.5 1.4 fusion.4015
  (1659 shorter events, 322.2 us)
Async XLA Ops:
  7.2 1.0 copy-start
  7.2 82.4 %all-reduce.261.cloned.1.call-start = ((), (), s32[]{:S(2)}) async-start(), calls=%async_computation.1 | async-start | bytes 655360 | tf_op jit(solution)/shard_map/psum | solution.py:45
  9.1 80.5 %copy-start.1 = (bf16[64,256]{1,0:T(8,128)(2,1)S(1)}, bf16[64,256]{1,0:T(8,128)(2,1)}, u32[]{:S(2)}) copy-start(bf16[64,256]{1,0:T(8,128)(2,1)} %param.5) | copy-start | bytes 98308
  13.2 908.5 %all-reduce.259.cloned.1.call-start = ((), (), s32[]{:S(2)}) async-start(), calls=%async_computation | async-start | bytes 1572864 | tf_op jit(solution)/shard_map/psum | solution.py:59
  297.0 208.3 %copy-start.3 = (f32[64,256]{1,0:T(8,128)S(1)}, f32[64,256]{1,0:T(8,128)}, u32[]{:S(2)}) copy-start(f32[64,256]{1,0:T(8,128)} %get-tuple-element.4) | copy-start | bytes 196612
  506.0 149.8 %copy-start.2 = (f32[64,256]{1,0:T(8,128)}, f32[64,256]{1,0:T(8,128)S(1)}, u32[]{:S(2)}) copy-start(f32[64,256]{1,0:T(8,128)S(1)} %get-tuple-element.777) | copy-start | bytes 196612
  1113.9 220.5 %copy-start.4 = (f32[512,256]{0,1:T(8,128)S(1)}, f32[512,256]{0,1:T(8,128)}, u32[]{:S(2)}) copy-start(f32[512,256]{0,1:T(8,128)} %get-tuple-element.2) | copy-start | bytes 1572868
Sparse Core Ops, SparseCore 0:
  13.3 76.1 all-reduce.260
  655.9 265.7 all-reduce.258
where the time goes:
time: 1360 us; the launch traced here: 1340 us
  between operations  512 us (38%)
  waiting for transfers between devices  342 us (25%)
  matrix products  168 us (12%)
  local copies, waits for them, and re-layouts  155 us (11%)
  blocking collectives  144 us (11%)
  other arithmetic  22.9 us (2%)
    psum x1, waiting for transfers between devices, local(): b_hat = solve_rows(second_gram, lax.psum(product, 'gx'))  266 us
    slice x256, local copies, waits for them, and re-layouts, lower_inverse(): w_top = lower_inverse(symmetric[:half, :half])  154 us
    psum x1, blocking collectives, local(): col_squares = lax.psum(jnp.sum(a_hat * a_hat, axis=0), 'gx')  144 us
    psum x1, waiting for transfers between devices, local(): b_gram, m_first = lax.psum((local_gram, first_part), 'gy')  76.3 us
    dot_general x254, matrix products, lower_inverse(): jnp.dot(w_bottom, jnp.dot(l_low, w_top, precision=lax.Precision.HIGHEST),...  53 us
    dot_general x254, matrix products, lower_inverse(): jnp.dot(l_low, w_top, precision=lax.Precision.HIGHEST)  43.7 us
    dot_general x254, matrix products, lower_inverse(): jnp.dot(symmetric[half:, :half], w_top.T, precision=lax.Precision.HIGHEST)  33.5 us
  transfers between devices with their start and end apart: 2, of which 2 were waited for; matrix products, arithmetic and copies ran while one was open for 0% of the time, Pallas kernels for 0%

commit v1 on v0

v1 whole, which is shorter than its diff:
```python
import functools

import jax
import jax.numpy as jnp
from jax import lax
from jax.experimental import pallas as pl
from jax.experimental.pallas import tpu as pltpu
from jax.sharding import Mesh
from jax.sharding import PartitionSpec as P

EPSILON = 1e-06
HIGH = lax.Precision.HIGHEST
BLOCK = 64
GROUP = 8
LANES = 128
PARTS = 8
STEPS = 12
RESIDUAL = 1e-8
VMEM_BYTES = 24 * 1024 * 1024
STREAM_BYTES = 115 * 512 * 1024
INVERSE_COST = pl.CostEstimate(flops=12_000_000_000, bytes_accessed=1_000_000, transcendentals=0)


def dot_nn(left, right):
    return lax.dot_general(left, right, (((1,), (0,)), ((), ())), precision=HIGH, preferred_element_type=jnp.float32)


def dot_tn(left, right):
    return lax.dot_general(left, right, (((0,), (0,)), ((), ())), precision=HIGH, preferred_element_type=jnp.float32)


def bf16_gram(factor):
    return lax.dot_general(factor, factor, (((0,), (0,)), ((), ())), preferred_element_type=jnp.float32)


def total(terms):
    terms = list(terms)
    while len(terms) > 1:
        paired = [terms[i] + terms[i + 1] for i in range(0, len(terms) - 1, 2)]
        terms = paired + ([terms[-1]] if len(terms) % 2 else [])
    return terms[0]


def solve_group(entries, rows):
    n = len(rows)
    e = [list(line) for line in entries]
    rows = list(rows)
    factors, scaled = {}, [None] * n
    for p in range(0, n, 2):
        a, b, c = e[p][p], e[p][p + 1], e[p + 1][p + 1]
        inv_det = pltpu.reciprocal(a * c - b * b, approx=True)
        inv_a, inv_b, inv_c = c * inv_det, b * inv_det, a * inv_det
        for i in range(p + 2, n):
            x, y = e[p][i], e[p + 1][i]
            f0, f1 = inv_a * x - inv_b * y, inv_c * y - inv_b * x
            factors[p, i] = f0, f1
            for j in range(i, n):
                e[i][j] = e[i][j] - (f0 * e[p][j] + f1 * e[p + 1][j])
            rows[i] = rows[i] - (f0 * rows[p] + f1 * rows[p + 1])
        scaled[p] = inv_a * rows[p] - inv_b * rows[p + 1]
        scaled[p + 1] = inv_c * rows[p + 1] - inv_b * rows[p]
    for p in range(n - 4, -1, -2):
        for q in range(2):
            scaled[p + q] = scaled[p + q] - total(factors[p, i][q] * scaled[i] for i in range(p + 2, n))
    return scaled


def block_inverse(block):
    order = block.shape[0]
    width = 2 * order
    count = order // GROUP
    eye = (
        lax.broadcasted_iota(jnp.int32, (order, order), 0) == lax.broadcasted_iota(jnp.int32, (order, order), 1)
    ).astype(jnp.float32)
    wide = jnp.concatenate([block, eye], axis=1)
    groups = [wide[g * GROUP : (g + 1) * GROUP] for g in range(count)]
    sub = lax.broadcasted_iota(jnp.int32, (GROUP, width), 0)
    full = (GROUP, width)
    for g in range(count):
        k = g * GROUP
        rows = [jnp.broadcast_to(groups[g][i : i + 1], full) for i in range(GROUP)]
        entries = [
            [jnp.broadcast_to(rows[i][:, k + j : k + j + 1], full) if j >= i else None for j in range(GROUP)]
            for i in range(GROUP)
        ]
        steps = solve_group(entries, rows)
        order_of = [h for h in range(g + 1, count)] + [h for h in range(g)]
        for h in order_of:
            cols = [jnp.broadcast_to(groups[h][:, k + j : k + j + 1], full) for j in range(GROUP)]
            groups[h] = groups[h] - total(cols[j] * steps[j] for j in range(GROUP))
        packed = steps[0]
        for i in range(1, GROUP):
            packed = jnp.where(sub == i, steps[i], packed)
        groups[g] = packed
    return jnp.concatenate([x[:, order:] for x in groups], axis=0)


def invert(work):
    order = work.shape[0]

    def sweep(_, carry):
        head = work[0:BLOCK, :]
        inv = block_inverse(head[:, 0:BLOCK])
        lane = lax.broadcasted_iota(jnp.int32, (BLOCK, order), 1)
        row = lax.broadcasted_iota(jnp.int32, (BLOCK, order), 0)
        band = dot_nn(inv, jnp.where(lane < BLOCK, (lane == row).astype(jnp.float32), head))
        rest = work[BLOCK:order, :]
        lane_low = lax.broadcasted_iota(jnp.int32, (order - BLOCK, order), 1)
        lower = jnp.where(lane_low < BLOCK, 0.0, rest) - dot_nn(rest[:, 0:BLOCK], band)
        work[0 : order - BLOCK, :] = pltpu.roll(lower, order - BLOCK, 1)
        work[order - BLOCK : order, :] = pltpu.roll(band, order - BLOCK, 1)
        return carry

    lax.fori_loop(0, order // BLOCK, sweep, 0)


def diagonal_mask(order):
    return lax.broadcasted_iota(jnp.int32, (order, order), 0) == lax.broadcasted_iota(jnp.int32, (order, order), 1)


def invert_scaled(matrix, work, inverse):
    order = matrix.shape[0]
    diagonal = diagonal_mask(order)
    kept = jnp.where(diagonal, matrix, 0.0)
    row = 1.0 / jnp.sqrt(jnp.sum(kept, axis=0, keepdims=True))
    col = 1.0 / jnp.sqrt(jnp.sum(kept, axis=1, keepdims=True))
    scaled = jnp.where(diagonal, 1.0, matrix * row * col)
    work[...] = scaled
    bound = jnp.max(jnp.sum(jnp.abs(scaled), axis=0, keepdims=True))
    size = jnp.where(bound < 2.0, 1.0, 1.0 / bound)
    inverse[...] = jnp.where(diagonal, 2.0 * size, 0.0) - (size * size) * scaled

    def unfinished(carry):
        residual, step = carry
        return (residual > RESIDUAL) & (step < STEPS)

    def improve(carry):
        step = carry[1]
        guess = inverse[...]
        error = jnp.where(diagonal_mask(order), 1.0, 0.0) - dot_nn(work[...], guess)
        inverse[...] = guess + dot_nn(guess, error)
        return jnp.sum(error * error), step + 1

    residual, _ = lax.while_loop(unfinished, improve, (jnp.float32(1.0), jnp.int32(0)))

    @pl.when(jnp.logical_not(residual <= RESIDUAL))
    def _():
        invert(work)
        inverse[...] = work[...]

    return row, col


def fetcher(source, kept, arrived):
    rows = source.shape[0] // PARTS

    def fetch(i):
        part = pl.ds(i * rows, rows)
        return pltpu.make_async_copy(source.at[part], kept.at[part], arrived.at[i])

    return fetch


def first_mode_kernel(tensor, factor_b, factor_c, out, kept, arrived):
    x_rows, time_len, depth = tensor.shape
    rank = factor_b.shape[1]
    rows, share = x_rows // PARTS, rank // PARTS

    fetch = fetcher(tensor, kept, arrived)
    for i in range(PARTS):
        fetch(i).start()
    gram = bf16_gram(factor_b[...])
    for i in range(PARTS):
        out[i, 0:share, :] = gram[i * share : (i + 1) * share]

    def contract(i, carry):
        fetch(i).wait()
        contracted = jnp.dot(
            kept[pl.ds(i * rows, rows)].reshape(rows * time_len, depth),
            factor_b[...],
            preferred_element_type=jnp.float32,
        ).reshape(rows, time_len, rank)
        out[i, share:, :] = jnp.sum(contracted * factor_c[...].astype(jnp.float32)[None], axis=1)
        return carry

    lax.fori_loop(0, PARTS, contract, 0)


def first_solve_kernel(where, gathered, factor_c, a_hat, slab, work, inverse, raw):
    rank = work.shape[0]
    share = rank // PARTS
    b_gram = jnp.concatenate([gathered[p, 0:share, :] for p in range(PARTS)], axis=0)
    m_first = jnp.concatenate([gathered[p, share:, :] for p in range(PARTS)], axis=0)
    row, _ = invert_scaled(b_gram * bf16_gram(factor_c[...]), work, inverse)
    rows = dot_nn(m_first * row, inverse[...]) * row
    a_hat[...] = rows
    raw[...] = dot_tn(rows, rows)
    mine = raw[pl.ds(where[0] * share, share), :]
    squares = jnp.sum(rows * rows, axis=0, keepdims=True)
    for p in range(PARTS):
        top, left = (p // 2) * GROUP, (p % 2) * LANES
        slab[p, 0:GROUP, :] = mine[top : top + GROUP, left : left + LANES]
        slab[p, GROUP:, :] = jnp.zeros((GROUP, LANES), jnp.float32)
        for h in range(rank // LANES):
            slab[p, GROUP + h : GROUP + h + 1, :] = squares[:, h * LANES : (h + 1) * LANES]


def assemble(pieces):
    bands = []
    for q in range(PARTS):
        for p in range(0, PARTS, 2):
            bands.append(jnp.concatenate([pieces[q, p], pieces[q, p + 1]], axis=1))
    return jnp.concatenate(bands, axis=0)


def norm_row(sums):
    squares = total(sums[p, GROUP:, :] for p in range(PARTS))
    return jnp.sqrt(jnp.concatenate([squares[0:1], squares[1:2]], axis=1) + EPSILON)


def second_mode_kernel(tensor, a_hat, sums, factor_c, out, kept, arrived):
    x_rows, time_len, depth = tensor.shape
    rank = a_hat.shape[1]
    rows, band = x_rows // PARTS, depth // PARTS
    fetch = fetcher(tensor, kept, arrived)
    for i in range(PARTS):
        fetch(i).start()
    norms = norm_row(sums)
    tile = total(sums[p, 0:GROUP, :] for p in range(PARTS))
    for p in range(PARTS):
        out[p, band:, 0:LANES] = tile
        out[p, band:, LANES:] = jnp.zeros((GROUP, rank - LANES), jnp.float32)
    out[:, 0:band, :] = jnp.zeros((PARTS, band, rank), jnp.float32)

    def contract(i, carry):
        fetch(i).wait()
        a_unit = a_hat[pl.ds(i * rows, rows), :] / norms
        khatri_rao = (a_unit[:, None, :] * factor_c[...].astype(jnp.float32)[None]).astype(jnp.bfloat16)
        out[:, 0:band, :] += lax.dot_general(
            kept[pl.ds(i * rows, rows)].reshape(rows * time_len, depth),
            khatri_rao.reshape(rows * time_len, rank),
            (((0,), (0,)), ((), ())),
            preferred_element_type=jnp.float32,
        ).reshape(PARTS, band, rank)
        return carry

    lax.fori_loop(0, PARTS, contract, 0)


def second_inverse_kernel(pieces, sums, factor_c, inverse, work):
    raw = assemble(pieces)
    norms = norm_row(sums)
    norms_down = jnp.sum(jnp.where(diagonal_mask(raw.shape[0]), norms, 0.0), axis=1, keepdims=True)
    row, col = invert_scaled(raw * bf16_gram(factor_c[...]), work, inverse)
    inverse[...] = inverse[...] * (row * norms) * (col * norms_down)


def second_solve_kernel(m_second, inverse, b_hat):
    b_hat[...] = dot_nn(total(m_second[p] for p in range(PARTS)), inverse[...])


def f32(*shape):
    return jax.ShapeDtypeStruct(shape, jnp.float32)


def call(kernel, out_shape, *operands, scratch=(), vmem=VMEM_BYTES, **more):
    return pl.pallas_call(
        kernel,
        out_shape=out_shape,
        scratch_shapes=list(scratch),
        compiler_params=pltpu.CompilerParams(vmem_limit_bytes=vmem),
        **more,
    )(*operands)


def scatter_sum(parts, axis):
    return jnp.sum(lax.all_to_all(parts, axis, 0, 0), axis=0)


def gather(block, axis):
    return lax.all_to_all(jnp.broadcast_to(block[None], (PARTS, *block.shape)), axis, 0, 0)


def local(tensor, factor_b, factor_c):
    x_rows, time_len, y_rows = tensor.shape
    rank = factor_b.shape[1]
    share = rank // PARTS
    x_step = x_rows // PARTS
    square = pltpu.VMEM((rank, rank), jnp.float32)

    whole = pl.BlockSpec(memory_space=pltpu.VMEM)
    streamed = dict(
        scratch=[pltpu.VMEM(tensor.shape, tensor.dtype), pltpu.SemaphoreType.DMA((PARTS,))], vmem=STREAM_BYTES
    )
    in_place = pl.BlockSpec(memory_space=pl.ANY)
    first = call(
        first_mode_kernel,
        f32(PARTS, share + x_step, rank),
        tensor,
        factor_b,
        factor_c,
        in_specs=[in_place, whole, whole],
        **streamed,
    )
    gathered = gather(scatter_sum(first, "gy"), "gy")

    where = lax.axis_index("gy").astype(jnp.int32).reshape(1)
    a_hat, slab = call(
        first_solve_kernel,
        (f32(x_rows, rank), f32(PARTS, 2 * GROUP, LANES)),
        where,
        gathered,
        factor_c,
        scratch=[square, square, square],
        in_specs=[pl.BlockSpec(memory_space=pltpu.SMEM), whole, whole],
    )

    sums = gather(scatter_sum(slab, "gl"), "gh")
    product = call(
        second_mode_kernel,
        f32(PARTS, y_rows // PARTS + GROUP, rank),
        tensor,
        a_hat,
        sums,
        factor_c,
        in_specs=[in_place, whole, whole, whole],
        **streamed,
    )
    received = lax.all_to_all(product, "gl", 0, 0)
    m_second = gather(jnp.sum(received[:, : y_rows // PARTS], axis=0), "gh")
    pieces = lax.all_gather(received[:, y_rows // PARTS :, :LANES], "gy")
    inverse = call(
        second_inverse_kernel, f32(rank, rank), pieces, sums, factor_c, scratch=[square], cost_estimate=INVERSE_COST
    )
    b_band = call(second_solve_kernel, f32(y_rows // PARTS, rank), m_second, inverse)
    b_hat = gather(b_band, "gl").reshape(y_rows, rank)
    return (a_hat, b_hat)


def solution(mesh):
    split = Mesh(mesh.devices.reshape(PARTS, PARTS, PARTS), ("gh", "gl", "gy"))
    x_axes = ("gh", "gl")
    return jax.shard_map(
        local,
        mesh=split,
        in_specs=(P(x_axes, None, "gy"), P("gy", None), P()),
        out_specs=(P(x_axes, None), P("gy", None)),
        check_vma=False,
    )
```

time: 1360 us -> 139 us (0.10)
  the two profiles are of different devices: /device:TPU:4 before, /device:TPU:64 now
where the time goes in v1:
time: 139 us; the launch traced here: 138 us
  blocking collectives  87.4 us (63%)
  Pallas kernels  26.4 us (19%)
  waiting for transfers between devices  11.9 us (9%)
  starting transfers between devices  9.03 us (6%)
  local copies, waits for them, and re-layouts  2.44 us (2%)
    all_to_all x2, blocking collectives, gather(): lax.all_to_all(jnp.broadcast_to(block[None], (PARTS, *block.shape)), axis...  37.4 us
    pallas_call x5, Pallas kernels, call(): pl.pallas_call(kernel, out_shape=out_shape, scratch_shapes=list(scratch),...  26.4 us
    all_to_all x2, blocking collectives, scatter_sum(): return jnp.sum(lax.all_to_all(parts, axis, 0, 0), axis=0)  24.5 us
    all_gather x1, blocking collectives, local(): pieces = lax.all_gather(received[:, y_rows // PARTS:, :LANES], 'gy')  12.8 us
    all_to_all x1, blocking collectives, local(): received = lax.all_to_all(product, 'gl', 0, 0)  12.6 us
    all_to_all x2, waiting for transfers between devices, gather(): lax.all_to_all(jnp.broadcast_to(block[None], (PARTS, *block.shape)), axis...  11.9 us
    all_to_all x2, starting transfers between devices, gather(): lax.all_to_all(jnp.broadcast_to(block[None], (PARTS, *block.shape)), axis...  9.03 us
  transfers between devices with their start and end apart: 2, of which 2 were waited for; matrix products, arithmetic and copies ran while one was open for 0% of the time, Pallas kernels for 8%

profile of v1, /device:TPU:64, one launch (start us, length us, event | category | flops | bytes accessed | tf_op | source)
XLA Modules:
  0.0 138.0 jit_solution(6181068502238093089)
XLA Ops:
  0.6 0.0 copy-start
  0.6 5.2 %shard_map.50 = f32[8,40,256]{2,1,0:T(8,128)} custom-call(bf16[64,64,512]{2,1,0:T(8,128)(2,1)} %tensor.3, bf16[512,256]{1,0:T(8,128)(2,1)} %factor_b.1, bf16[64,256]{1,0:T(8,128)(2,1)} %factor_c.7), custom_call_target="tpu_custom_call" | custom-call | tf_op jit(solution)/shard_map/pallas_call | solution.py:267
  5.9 12.6 %all_to_all.35 = f32[8,40,256]{2,1,0:T(8,128)S(1)} all-to-all(f32[8,40,256]{2,1,0:T(8,128)} %shard_map.50), channel_id=1, replica_groups=mesh['gh'=8,'gl'=8,'gy'=8] {'gy'}, dimensions={0} | all-to-all | bytes 655360 | tf_op jit(solution)/shard_map/all_to_all | solution.py:277
  18.5 0.7 broadcast_in_dim.8
  19.2 3.4 %all-to-all-start.1 = ((f32[8,40,256]{2,1,0:T(8,128)}), f32[8,40,256]{2,1,0:T(8,128)S(1)}, u32[]{:S(2)}, u32[]{:S(2)}) async-start(f32[8,40,256]{2,1,0:T(8,128)} %broadcast_in_dim.8), calls=%async_computation.1 | async-start | bytes 655360 | tf_op jit(solution)/shard_map/all_to_all | solution.py:281
  22.7 8.2 %all-to-all-done.1.gathered = f32[8,40,256]{2,1,0:T(8,128)S(1)} async-done(((f32[8,40,256]{2,1,0:T(8,128)}), f32[8,40,256]{2,1,0:T(8,128)S(1)}, u32[]{:S(2)}, u32[]{:S(2)}) %all-to-all-start.1) | async-done | bytes 327712 | tf_op jit(solution)/shard_map/all_to_all | solution.py:281
  30.8 0.0 copy-done
  30.8 4.8 %shard_map.51 = (f32[64,256]{1,0:T(8,128)}, f32[8,16,128]{2,1,0:T(8,128)S(1)}) custom-call(s32[1]{0:T(128)} %bitcast.where, f32[8,40,256]{2,1,0:T(8,128)S(1)} %all-to-all-done.1.gathered, bf16[64,256]{1,0:T(8,128)(2,1)S(1)} %copy-done), custom_call_target="tpu_custom_call" | custom-call | tf_op jit(solution)/shard_map/pallas_call | solution.py:267
  35.6 11.9 %all_to_all.36 = f32[8,16,128]{2,1,0:T(8,128)S(1)} all-to-all(f32[8,16,128]{2,1,0:T(8,128)S(1)} %get-tuple-element.5), channel_id=1, replica_groups=mesh['gh'=8,'gl'=8,'gy'=8] {'gl'}, dimensions={0} | all-to-all | bytes 131072 | tf_op jit(solution)/shard_map/all_to_all | solution.py:277
  47.6 24.9 %all_to_all.37.sums = f32[8,16,128]{2,1,0:T(8,128)} all-to-all(f32[8,16,128]{2,1,0:T(8,128)S(1)} %broadcast_in_dim.9), channel_id=1, replica_groups=mesh['gh'=8,'gl'=8,'gy'=8] {'gh'}, dimensions={0} | all-to-all | bytes 131072 | tf_op jit(solution)/shard_map/all_to_all | solution.py:281
  72.5 0.0 copy-start.1
  72.5 0.0 copy-start.2
  72.5 5.6 %shard_map.52 = f32[8,72,256]{2,1,0:T(8,128)} custom-call(bf16[64,64,512]{2,1,0:T(8,128)(2,1)} %tensor.3, f32[64,256]{1,0:T(8,128)} %get-tuple-element.8.a_hat, f32[8,16,128]{2,1,0:T(8,128)} %all_to_all.37.sums, bf16[64,256]{1,0:T(8,128)(2,1)} %factor_c.7), custom_call_target="tpu_custom_call" | custom-call | tf_op jit(solution)/shard_map/pallas_call | solution.py:267
  78.2 12.6 %all_to_all.38 = f32[8,72,256]{2,1,0:T(8,128)S(1)} all-to-all(f32[8,72,256]{2,1,0:T(8,128)} %shard_map.52), channel_id=1, replica_groups=mesh['gh'=8,'gl'=8,'gy'=8] {'gl'}, dimensions={0} | all-to-all | bytes 1179648 | tf_op jit(solution)/shard_map/all_to_all | solution.py:329
  90.8 0.8 broadcast_in_dim.10
  91.7 5.6 %all-to-all-start.5 = ((f32[8,64,256]{2,1,0:T(8,128)}), f32[8,64,256]{2,1,0:T(8,128)S(1)}, u32[]{:S(2)}, u32[]{:S(2)}) async-start(f32[8,64,256]{2,1,0:T(8,128)} %broadcast_in_dim.10), calls=%async_computation.5 | async-start | bytes 1048576 | tf_op jit(solution)/shard_map/all_to_all | solution.py:281
  97.2 12.8 %all-gather = f32[64,8,128]{2,1,0:T(8,128)S(1)} all-gather(f32[8,8,128]{2,1,0:T(8,128)S(1)} %slice.9), channel_id=2, replica_groups=mesh['gh'=8,'gl'=8,'gy'=8] {'gy'}, dimensions={0}, use_global_device_ids=true | all-gather | bytes 294912 | tf_op jit(solution)/shard_map/all_gather | solution.py:331
  110.1 0.0 copy-done.1
  110.1 0.0 copy-done.2
  110.1 10.5 %shard_map.53.inverse = f32[256,256]{1,0:T(8,128)S(1)} custom-call(f32[8,8,8,128]{3,2,1,0:T(8,128)S(1)} %bitcast.3, f32[8,16,128]{2,1,0:T(8,128)S(1)} %copy-done.2, bf16[64,256]{1,0:T(8,128)(2,1)S(1)} %copy-done.1), custom_call_target="tpu_custom_call" | custom-call | flops 12000000000 | bytes 1000000 | tf_op jit(solution)/shard_map/pallas_call | solution.py:267
  120.6 3.8 %all-to-all-done.5.m_second = f32[8,64,256]{2,1,0:T(8,128)S(1)} async-done(((f32[8,64,256]{2,1,0:T(8,128)}), f32[8,64,256]{2,1,0:T(8,128)S(1)}, u32[]{:S(2)}, u32[]{:S(2)}) %all-to-all-start.5) | async-done | bytes 524320 | tf_op jit(solution)/shard_map/all_to_all | solution.py:281
  124.4 0.3 shard_map.54
  124.7 12.5 %all_to_all.39 = f32[8,64,256]{2,1,0:T(8,128)S(1)} all-to-all(f32[8,64,256]{2,1,0:T(8,128)S(1)} %broadcast_in_dim.11), channel_id=1, replica_groups=mesh['gh'=8,'gl'=8,'gy'=8] {'gl'}, dimensions={0} | all-to-all | bytes 1048576 | tf_op jit(solution)/shard_map/all_to_all | solution.py:281
  137.2 0.8 copy.6
  (6 shorter events, 0.1 us)
Async XLA Ops:
  0.6 30.2 %copy-start = (bf16[64,256]{1,0:T(8,128)(2,1)S(1)}, bf16[64,256]{1,0:T(8,128)(2,1)}, u32[]{:S(2)}) copy-start(bf16[64,256]{1,0:T(8,128)(2,1)} %factor_c.7) | copy-start | bytes 98308
  19.2 11.6 %all-to-all-start.1 = ((f32[8,40,256]{2,1,0:T(8,128)}), f32[8,40,256]{2,1,0:T(8,128)S(1)}, u32[]{:S(2)}, u32[]{:S(2)}) async-start(f32[8,40,256]{2,1,0:T(8,128)} %broadcast_in_dim.8), calls=%async_computation.1 | async-start | bytes 655360 | tf_op jit(solution)/shard_map/all_to_all | solution.py:281
  72.5 37.5 %copy-start.1 = (bf16[64,256]{1,0:T(8,128)(2,1)S(1)}, bf16[64,256]{1,0:T(8,128)(2,1)}, u32[]{:S(2)}) copy-start(bf16[64,256]{1,0:T(8,128)(2,1)} %factor_c.7) | copy-start | bytes 98308
  72.5 37.5 %copy-start.2 = (f32[8,16,128]{2,1,0:T(8,128)S(1)}, f32[8,16,128]{2,1,0:T(8,128)}, u32[]{:S(2)}) copy-start(f32[8,16,128]{2,1,0:T(8,128)} %all_to_all.37.sums) | copy-start | bytes 196612
  91.7 32.7 %all-to-all-start.5 = ((f32[8,64,256]{2,1,0:T(8,128)}), f32[8,64,256]{2,1,0:T(8,128)S(1)}, u32[]{:S(2)}, u32[]{:S(2)}) async-start(f32[8,64,256]{2,1,0:T(8,128)} %broadcast_in_dim.10), calls=%async_computation.5 | async-start | bytes 1048576 | tf_op jit(solution)/shard_map/all_to_all | solution.py:281

commit v2 on v1

--- a/solution.py
+++ b/solution.py
@@ -13,6 +13,8 @@
 BLOCK = 64
 GROUP = 8
 LANES = 128
+JOINED = 2
+SLOTS = 5
 PARTS = 8
 STEPS = 12
 RESIDUAL = 1e-8
@@ -151,36 +153,76 @@
     return row, col
 
 
-def fetcher(source, kept, arrived):
+def fetch_parts(source, kept, arrived):
     rows = source.shape[0] // PARTS
 
-    def fetch(i):
+    def copy(i):
         part = pl.ds(i * rows, rows)
         return pltpu.make_async_copy(source.at[part], kept.at[part], arrived.at[i])
 
-    return fetch
-
-
-def first_mode_kernel(tensor, factor_b, factor_c, out, kept, arrived):
+    for i in range(PARTS):
+        copy(i).start()
+    return lambda i: copy(i).wait()
+
+
+def fetch_small(sources, targets, arrived):
+    copies = [pltpu.make_async_copy(s, t, arrived.at[n]) for n, (s, t) in enumerate(zip(sources, targets))]
+    for one in copies:
+        one.start()
+    return copies
+
+
+def packed_gram(gram):
+    low = lax.broadcasted_iota(jnp.int32, (BLOCK, LANES), 1) < BLOCK
+    return [
+        gram[0:64, 0:128],
+        gram[128:192, 0:128],
+        gram[192:256, 0:128],
+        gram[192:256, 128:256],
+        jnp.where(low, gram[128:192, 128:256], gram[64:128, 0:128]),
+    ]
+
+
+def unpacked_gram(slots):
+    low = lax.broadcasted_iota(jnp.int32, (BLOCK, LANES), 1) < BLOCK
+    none = jnp.zeros((BLOCK, LANES), jnp.float32)
+    half = jnp.concatenate(
+        [
+            jnp.concatenate([slots[0], none], axis=1),
+            jnp.concatenate([jnp.where(low, 0.0, slots[4]), none], axis=1),
+            jnp.concatenate([slots[1], jnp.where(low, slots[4], 0.0)], axis=1),
+            jnp.concatenate([slots[2], slots[3]], axis=1),
+        ],
+        axis=0,
+    )
+    shape = half.shape
+    row_block = lax.broadcasted_iota(jnp.int32, shape, 0) // BLOCK
+    col_block = lax.broadcasted_iota(jnp.int32, shape, 1) // BLOCK
+    return half + jnp.where(row_block == col_block, 0.0, half).T
+
+
+def first_mode_kernel(tensor_in, factor_b_in, factor_c_in, out, tensor, factor_b, factor_c, arrived, arrived_small):
     x_rows, time_len, depth = tensor.shape
     rank = factor_b.shape[1]
-    rows, share = x_rows // PARTS, rank // PARTS
-
-    fetch = fetcher(tensor, kept, arrived)
-    for i in range(PARTS):
-        fetch(i).start()
-    gram = bf16_gram(factor_b[...])
-    for i in range(PARTS):
-        out[i, 0:share, :] = gram[i * share : (i + 1) * share]
+    rows = x_rows // PARTS
+    small = fetch_small([factor_b_in, factor_c_in], [factor_b, factor_c], arrived_small)
+    wait_part = fetch_parts(tensor_in, tensor, arrived)
+    for one in small:
+        one.wait()
+    for t, slot in enumerate(packed_gram(bf16_gram(factor_b[...]))):
+        for i in range(PARTS):
+            out[i, t * GROUP : (t + 1) * GROUP, :] = slot[i * GROUP : (i + 1) * GROUP]
 
     def contract(i, carry):
-        fetch(i).wait()
+        wait_part(i)
         contracted = jnp.dot(
-            kept[pl.ds(i * rows, rows)].reshape(rows * time_len, depth),
+            tensor[pl.ds(i * rows, rows)].reshape(rows * time_len, depth),
             factor_b[...],
             preferred_element_type=jnp.float32,
         ).reshape(rows, time_len, rank)
-        out[i, share:, :] = jnp.sum(contracted * factor_c[...].astype(jnp.float32)[None], axis=1)
+        summed = jnp.sum(contracted * factor_c[...].astype(jnp.float32)[None], axis=1)
+        for h in range(rank // LANES):
+            out[i, pl.ds((SLOTS + h) * GROUP, rows), :] = summed[:, h * LANES : (h + 1) * LANES]
         return carry
 
     lax.fori_loop(0, PARTS, contract, 0)
@@ -189,8 +231,12 @@
 def first_solve_kernel(where, gathered, factor_c, a_hat, slab, work, inverse, raw):
     rank = work.shape[0]
     share = rank // PARTS
-    b_gram = jnp.concatenate([gathered[p, 0:share, :] for p in range(PARTS)], axis=0)
-    m_first = jnp.concatenate([gathered[p, share:, :] for p in range(PARTS)], axis=0)
+    bands = [
+        jnp.concatenate([gathered[p, t * GROUP : (t + 1) * GROUP, :] for p in range(PARTS)], axis=0)
+        for t in range(SLOTS + rank // LANES)
+    ]
+    b_gram = unpacked_gram(bands[:SLOTS])
+    m_first = jnp.concatenate(bands[SLOTS:], axis=1)
     row, _ = invert_scaled(b_gram * bf16_gram(factor_c[...]), work, inverse)
     rows = dot_nn(m_first * row, inverse[...]) * row
     a_hat[...] = rows
@@ -218,13 +264,16 @@
     return jnp.sqrt(jnp.concatenate([squares[0:1], squares[1:2]], axis=1) + EPSILON)
 
 
-def second_mode_kernel(tensor, a_hat, sums, factor_c, out, kept, arrived):
+def second_mode_kernel(
+    tensor_in, a_hat_in, sums_in, factor_c_in, out, tensor, a_hat, sums, factor_c, arrived, arrived_small
+):
     x_rows, time_len, depth = tensor.shape
     rank = a_hat.shape[1]
-    rows, band = x_rows // PARTS, depth // PARTS
-    fetch = fetcher(tensor, kept, arrived)
-    for i in range(PARTS):
-        fetch(i).start()
+    rows, band = JOINED * x_rows // PARTS, depth // PARTS
+    small = fetch_small([sums_in, a_hat_in, factor_c_in], [sums, a_hat, factor_c], arrived_small)
+    wait_part = fetch_parts(tensor_in, tensor, arrived)
+    for one in small:
+        one.wait()
     norms = norm_row(sums)
     tile = total(sums[p, 0:GROUP, :] for p in range(PARTS))
     for p in range(PARTS):
@@ -233,18 +282,19 @@
     out[:, 0:band, :] = jnp.zeros((PARTS, band, rank), jnp.float32)
 
     def contract(i, carry):
-        fetch(i).wait()
+        for n in range(JOINED):
+            wait_part(i * JOINED + n)
         a_unit = a_hat[pl.ds(i * rows, rows), :] / norms
         khatri_rao = (a_unit[:, None, :] * factor_c[...].astype(jnp.float32)[None]).astype(jnp.bfloat16)
         out[:, 0:band, :] += lax.dot_general(
-            kept[pl.ds(i * rows, rows)].reshape(rows * time_len, depth),
+            tensor[pl.ds(i * rows, rows)].reshape(rows * time_len, depth),
             khatri_rao.reshape(rows * time_len, rank),
             (((0,), (0,)), ((), ())),
             preferred_element_type=jnp.float32,
         ).reshape(PARTS, band, rank)
         return carry
 
-    lax.fori_loop(0, PARTS, contract, 0)
+    lax.fori_loop(0, PARTS // JOINED, contract, 0)
 
 
 def second_inverse_kernel(pieces, sums, factor_c, inverse, work):
@@ -273,6 +323,21 @@
     )(*operands)
 
 
+def stream(kernel, out_shape, *operands):
+    return call(
+        kernel,
+        out_shape,
+        *operands,
+        scratch=[
+            *(pltpu.VMEM(x.shape, x.dtype) for x in operands),
+            pltpu.SemaphoreType.DMA((PARTS,)),
+            pltpu.SemaphoreType.DMA((len(operands) - 1,)),
+        ],
+        vmem=STREAM_BYTES,
+        in_specs=[pl.BlockSpec(memory_space=pl.ANY)] * len(operands),
+    )
+
+
 def scatter_sum(parts, axis):
     return jnp.sum(lax.all_to_all(parts, axis, 0, 0), axis=0)
 
@@ -284,23 +349,11 @@
 def local(tensor, factor_b, factor_c):
     x_rows, time_len, y_rows = tensor.shape
     rank = factor_b.shape[1]
-    share = rank // PARTS
-    x_step = x_rows // PARTS
     square = pltpu.VMEM((rank, rank), jnp.float32)
 
     whole = pl.BlockSpec(memory_space=pltpu.VMEM)
-    streamed = dict(
-        scratch=[pltpu.VMEM(tensor.shape, tensor.dtype), pltpu.SemaphoreType.DMA((PARTS,))], vmem=STREAM_BYTES
-    )
-    in_place = pl.BlockSpec(memory_space=pl.ANY)
-    first = call(
-        first_mode_kernel,
-        f32(PARTS, share + x_step, rank),
-        tensor,
-        factor_b,
-        factor_c,
-        in_specs=[in_place, whole, whole],
-        **streamed,
+    first = stream(
+        first_mode_kernel, f32(PARTS, (SLOTS + rank // LANES) * GROUP, LANES), tensor, factor_b, factor_c
     )
     gathered = gather(scatter_sum(first, "gy"), "gy")
 
@@ -316,15 +369,8 @@
     )
 
     sums = gather(scatter_sum(slab, "gl"), "gh")
-    product = call(
-        second_mode_kernel,
-        f32(PARTS, y_rows // PARTS + GROUP, rank),
-        tensor,
-        a_hat,
-        sums,
-        factor_c,
-        in_specs=[in_place, whole, whole, whole],
-        **streamed,
+    product = stream(
+        second_mode_kernel, f32(PARTS, y_rows // PARTS + GROUP, rank), tensor, a_hat, sums, factor_c
     )
     received = lax.all_to_all(product, "gl", 0, 0)
     m_second = gather(jnp.sum(received[:, : y_rows // PARTS], axis=0), "gh")

time: 139 us -> 135 us (0.971)
  Pallas kernels: 26.4 us -> 24.9 us
    pallas_call x5, Pallas kernels: 26.4 us -> 24.9 us  [call(): pl.pallas_call(kernel, out_shape=out_shape, scratch_shapes=list(scratch),...]
where the time goes in v2:
time: 135 us; the launch traced here: 134 us
  blocking collectives  86.4 us (64%)
  Pallas kernels  24.9 us (18%)
  waiting for transfers between devices  11 us (8%)
  starting transfers between devices  8.99 us (7%)
  local copies, waits for them, and re-layouts  2.4 us (2%)
    all_to_all x2, blocking collectives, gather(): lax.all_to_all(jnp.broadcast_to(block[None], (PARTS, *block.shape)), axis...  37.5 us
    pallas_call x5, Pallas kernels, call(): pl.pallas_call(kernel, out_shape=out_shape, scratch_shapes=list(scratch),...  24.9 us
    all_to_all x2, blocking collectives, scatter_sum(): return jnp.sum(lax.all_to_all(parts, axis, 0, 0), axis=0)  23.5 us
    all_gather x1, blocking collectives, local(): pieces = lax.all_gather(received[:, y_rows // PARTS:, :LANES], 'gy')  12.8 us
    all_to_all x1, blocking collectives, local(): received = lax.all_to_all(product, 'gl', 0, 0)  12.6 us
    all_to_all x2, waiting for transfers between devices, gather(): lax.all_to_all(jnp.broadcast_to(block[None], (PARTS, *block.shape)), axis...  11 us
    all_to_all x2, starting transfers between devices, gather(): lax.all_to_all(jnp.broadcast_to(block[None], (PARTS, *block.shape)), axis...  8.99 us
  transfers between devices with their start and end apart: 2, of which 2 were waited for; matrix products, arithmetic and copies ran while one was open for 0% of the time, Pallas kernels for 8%

profile of v2, /device:TPU:64, one launch (start us, length us, event | category | flops | bytes accessed | tf_op | source)
XLA Modules:
  0.0 134.4 jit_solution(12246286506956055965)
XLA Ops:
  0.6 0.0 copy-start
  0.6 5.5 %shard_map.50 = f32[8,56,128]{2,1,0:T(8,128)} custom-call(bf16[64,64,512]{2,1,0:T(8,128)(2,1)} %tensor_in.3, bf16[512,256]{1,0:T(8,128)(2,1)} %factor_b_in.1, bf16[64,256]{1,0:T(8,128)(2,1)} %factor_c.3), custom_call_target="tpu_custom_call" | custom-call | tf_op jit(solution)/shard_map/pallas_call | solution.py:317
  6.1 11.5 %all_to_all.35 = f32[8,56,128]{2,1,0:T(8,128)S(1)} all-to-all(f32[8,56,128]{2,1,0:T(8,128)} %shard_map.50), channel_id=1, replica_groups=mesh['gh'=8,'gl'=8,'gy'=8] {'gy'}, dimensions={0} | all-to-all | bytes 458752 | tf_op jit(solution)/shard_map/all_to_all | solution.py:342
  17.7 0.7 broadcast_in_dim.8
  18.4 3.4 %all-to-all-start.1 = ((f32[8,56,128]{2,1,0:T(8,128)}), f32[8,56,128]{2,1,0:T(8,128)S(1)}, u32[]{:S(2)}, u32[]{:S(2)}) async-start(f32[8,56,128]{2,1,0:T(8,128)} %broadcast_in_dim.8), calls=%async_computation.1 | async-start | bytes 458752 | tf_op jit(solution)/shard_map/all_to_all | solution.py:346
  21.8 7.1 %all-to-all-done.1.gathered = f32[8,56,128]{2,1,0:T(8,128)S(1)} async-done(((f32[8,56,128]{2,1,0:T(8,128)}), f32[8,56,128]{2,1,0:T(8,128)S(1)}, u32[]{:S(2)}, u32[]{:S(2)}) %all-to-all-start.1) | async-done | bytes 229408 | tf_op jit(solution)/shard_map/all_to_all | solution.py:346
  28.9 0.0 copy-done
  28.9 3.7 %shard_map.51 = (f32[64,256]{1,0:T(8,128)}, f32[8,16,128]{2,1,0:T(8,128)S(1)}) custom-call(s32[1]{0:T(128)} %bitcast.where, f32[8,56,128]{2,1,0:T(8,128)S(1)} %all-to-all-done.1.gathered, bf16[64,256]{1,0:T(8,128)(2,1)S(1)} %copy-done), custom_call_target="tpu_custom_call" | custom-call | tf_op jit(solution)/shard_map/pallas_call | solution.py:317
  32.6 11.9 %all_to_all.36 = f32[8,16,128]{2,1,0:T(8,128)S(1)} all-to-all(f32[8,16,128]{2,1,0:T(8,128)S(1)} %get-tuple-element.5), channel_id=1, replica_groups=mesh['gh'=8,'gl'=8,'gy'=8] {'gl'}, dimensions={0} | all-to-all | bytes 131072 | tf_op jit(solution)/shard_map/all_to_all | solution.py:342
  44.6 24.9 %all_to_all.37.sums_in.sums = f32[8,16,128]{2,1,0:T(8,128)} all-to-all(f32[8,16,128]{2,1,0:T(8,128)S(1)} %broadcast_in_dim.9), channel_id=1, replica_groups=mesh['gh'=8,'gl'=8,'gy'=8] {'gh'}, dimensions={0} | all-to-all | bytes 131072 | tf_op jit(solution)/shard_map/all_to_all | solution.py:346
  69.5 0.0 copy-start.1
  69.5 0.0 copy-start.2
  69.5 4.9 %shard_map.52 = f32[8,72,256]{2,1,0:T(8,128)} custom-call(bf16[64,64,512]{2,1,0:T(8,128)(2,1)} %tensor_in.3, f32[64,256]{1,0:T(8,128)} %get-tuple-element.8.a_hat_in, f32[8,16,128]{2,1,0:T(8,128)} %all_to_all.37.sums_in.sums, bf16[64,256]{1,0:T(8,128)(2,1)} %factor_c.3), custom_call_target="tpu_custom_call" | custom-call | tf_op jit(solution)/shard_map/pallas_call | solution.py:317
  74.4 12.6 %all_to_all.38 = f32[8,72,256]{2,1,0:T(8,128)S(1)} all-to-all(f32[8,72,256]{2,1,0:T(8,128)} %shard_map.52), channel_id=1, replica_groups=mesh['gh'=8,'gl'=8,'gy'=8] {'gl'}, dimensions={0} | all-to-all | bytes 1179648 | tf_op jit(solution)/shard_map/all_to_all | solution.py:375
  87.1 0.8 broadcast_in_dim.10
  87.9 5.6 %all-to-all-start.5 = ((f32[8,64,256]{2,1,0:T(8,128)}), f32[8,64,256]{2,1,0:T(8,128)S(1)}, u32[]{:S(2)}, u32[]{:S(2)}) async-start(f32[8,64,256]{2,1,0:T(8,128)} %broadcast_in_dim.10), calls=%async_computation.5 | async-start | bytes 1048576 | tf_op jit(solution)/shard_map/all_to_all | solution.py:346
  93.5 12.8 %all-gather = f32[64,8,128]{2,1,0:T(8,128)S(1)} all-gather(f32[8,8,128]{2,1,0:T(8,128)S(1)} %slice.9), channel_id=2, replica_groups=mesh['gh'=8,'gl'=8,'gy'=8] {'gy'}, dimensions={0}, use_global_device_ids=true | all-gather | bytes 294912 | tf_op jit(solution)/shard_map/all_gather | solution.py:377
  106.3 0.0 copy-done.1
  106.3 0.0 copy-done.2
  106.3 10.5 %shard_map.53.inverse = f32[256,256]{1,0:T(8,128)S(1)} custom-call(f32[8,8,8,128]{3,2,1,0:T(8,128)S(1)} %bitcast.3, f32[8,16,128]{2,1,0:T(8,128)S(1)} %copy-done.2, bf16[64,256]{1,0:T(8,128)(2,1)S(1)} %copy-done.1), custom_call_target="tpu_custom_call" | custom-call | flops 12000000000 | bytes 1000000 | tf_op jit(solution)/shard_map/pallas_call | solution.py:317
  116.8 3.9 %all-to-all-done.5.m_second = f32[8,64,256]{2,1,0:T(8,128)S(1)} async-done(((f32[8,64,256]{2,1,0:T(8,128)}), f32[8,64,256]{2,1,0:T(8,128)S(1)}, u32[]{:S(2)}, u32[]{:S(2)}) %all-to-all-start.5) | async-done | bytes 524320 | tf_op jit(solution)/shard_map/all_to_all | solution.py:346
  120.7 0.3 shard_map.54
  121.0 12.6 %all_to_all.39 = f32[8,64,256]{2,1,0:T(8,128)S(1)} all-to-all(f32[8,64,256]{2,1,0:T(8,128)S(1)} %broadcast_in_dim.11), channel_id=1, replica_groups=mesh['gh'=8,'gl'=8,'gy'=8] {'gl'}, dimensions={0} | all-to-all | bytes 1048576 | tf_op jit(solution)/shard_map/all_to_all | solution.py:346
  133.6 0.8 copy.6
  (6 shorter events, 0.1 us)
Async XLA Ops:
  0.6 28.3 %copy-start = (bf16[64,256]{1,0:T(8,128)(2,1)S(1)}, bf16[64,256]{1,0:T(8,128)(2,1)}, u32[]{:S(2)}) copy-start(bf16[64,256]{1,0:T(8,128)(2,1)} %factor_c.3) | copy-start | bytes 98308
  18.4 10.5 %all-to-all-start.1 = ((f32[8,56,128]{2,1,0:T(8,128)}), f32[8,56,128]{2,1,0:T(8,128)S(1)}, u32[]{:S(2)}, u32[]{:S(2)}) async-start(f32[8,56,128]{2,1,0:T(8,128)} %broadcast_in_dim.8), calls=%async_computation.1 | async-start | bytes 458752 | tf_op jit(solution)/shard_map/all_to_all | solution.py:346
  69.5 36.8 %copy-start.1 = (bf16[64,256]{1,0:T(8,128)(2,1)S(1)}, bf16[64,256]{1,0:T(8,128)(2,1)}, u32[]{:S(2)}) copy-start(bf16[64,256]{1,0:T(8,128)(2,1)} %factor_c.3) | copy-start | bytes 98308
  69.5 36.8 %copy-start.2 = (f32[8,16,128]{2,1,0:T(8,128)S(1)}, f32[8,16,128]{2,1,0:T(8,128)}, u32[]{:S(2)}) copy-start(f32[8,16,128]{2,1,0:T(8,128)} %all_to_all.37.sums_in.sums) | copy-start | bytes 196612
  87.9 32.8 %all-to-all-start.5 = ((f32[8,64,256]{2,1,0:T(8,128)}), f32[8,64,256]{2,1,0:T(8,128)S(1)}, u32[]{:S(2)}, u32[]{:S(2)}) async-start(f32[8,64,256]{2,1,0:T(8,128)} %broadcast_in_dim.10), calls=%async_computation.5 | async-start | bytes 1048576 | tf_op jit(solution)/shard_map/all_to_all | solution.py:346

commit v3 on v2

--- a/solution.py
+++ b/solution.py
@@ -16,6 +16,7 @@
 JOINED = 2
 SLOTS = 5
 PARTS = 8
+AHEAD = 2
 STEPS = 12
 RESIDUAL = 1e-8
 VMEM_BYTES = 24 * 1024 * 1024
@@ -143,7 +144,10 @@
         inverse[...] = guess + dot_nn(guess, error)
         return jnp.sum(error * error), step + 1
 
-    residual, _ = lax.while_loop(unfinished, improve, (jnp.float32(1.0), jnp.int32(0)))
+    carry = (jnp.float32(1.0), jnp.int32(0))
+    for _ in range(2):
+        carry = improve(carry)
+    residual, _ = lax.while_loop(unfinished, improve, carry)
 
     @pl.when(jnp.logical_not(residual <= RESIDUAL))
     def _():
@@ -153,23 +157,23 @@
     return row, col
 
 
-def fetch_parts(source, kept, arrived):
-    rows = source.shape[0] // PARTS
+def fetch(tensor_in, tensor, small_in, small, arrived, arrived_small):
+    rows = tensor.shape[0] // PARTS
 
     def copy(i):
         part = pl.ds(i * rows, rows)
-        return pltpu.make_async_copy(source.at[part], kept.at[part], arrived.at[i])
-
-    for i in range(PARTS):
+        return pltpu.make_async_copy(tensor_in.at[part], tensor.at[part], arrived.at[i])
+
+    copies = [pltpu.make_async_copy(s, t, arrived_small.at[n]) for n, (s, t) in enumerate(zip(small_in, small))]
+    for one in copies:
+        one.start()
+    for i in range(AHEAD):
+        copy(i).start()
+    for one in copies:
+        one.wait()
+    for i in range(AHEAD, PARTS):
         copy(i).start()
     return lambda i: copy(i).wait()
-
-
-def fetch_small(sources, targets, arrived):
-    copies = [pltpu.make_async_copy(s, t, arrived.at[n]) for n, (s, t) in enumerate(zip(sources, targets))]
-    for one in copies:
-        one.start()
-    return copies
 
 
 def packed_gram(gram):
@@ -205,10 +209,9 @@
     x_rows, time_len, depth = tensor.shape
     rank = factor_b.shape[1]
     rows = x_rows // PARTS
-    small = fetch_small([factor_b_in, factor_c_in], [factor_b, factor_c], arrived_small)
-    wait_part = fetch_parts(tensor_in, tensor, arrived)
-    for one in small:
-        one.wait()
+    wait_part = fetch(
+        tensor_in, tensor, [factor_b_in, factor_c_in], [factor_b, factor_c], arrived, arrived_small
+    )
     for t, slot in enumerate(packed_gram(bf16_gram(factor_b[...]))):
         for i in range(PARTS):
             out[i, t * GROUP : (t + 1) * GROUP, :] = slot[i * GROUP : (i + 1) * GROUP]
@@ -270,10 +273,9 @@
     x_rows, time_len, depth = tensor.shape
     rank = a_hat.shape[1]
     rows, band = JOINED * x_rows // PARTS, depth // PARTS
-    small = fetch_small([sums_in, a_hat_in, factor_c_in], [sums, a_hat, factor_c], arrived_small)
-    wait_part = fetch_parts(tensor_in, tensor, arrived)
-    for one in small:
-        one.wait()
+    wait_part = fetch(
+        tensor_in, tensor, [sums_in, a_hat_in, factor_c_in], [sums, a_hat, factor_c], arrived, arrived_small
+    )
     norms = norm_row(sums)
     tile = total(sums[p, 0:GROUP, :] for p in range(PARTS))
     for p in range(PARTS):

time: 135 us -> 134 us (level)
  no operation moved by 1% of the time
where the time goes in v3:
time: 134 us
  blocking collectives  86.4 us (64%)
  Pallas kernels  23.9 us (18%)
  waiting for transfers between devices  11 us (8%)
  starting transfers between devices  8.99 us (7%)
  local copies, waits for them, and re-layouts  2.4 us (2%)
    all_to_all x2, blocking collectives, gather(): lax.all_to_all(jnp.broadcast_to(block[None], (PARTS, *block.shape)), axis...  37.5 us
    pallas_call x5, Pallas kernels, call(): pl.pallas_call(kernel, out_shape=out_shape, scratch_shapes=list(scratch),...  23.9 us
    all_to_all x2, blocking collectives, scatter_sum(): return jnp.sum(lax.all_to_all(parts, axis, 0, 0), axis=0)  23.5 us
    all_gather x1, blocking collectives, local(): pieces = lax.all_gather(received[:, y_rows // PARTS:, :LANES], 'gy')  12.8 us
    all_to_all x1, blocking collectives, local(): received = lax.all_to_all(product, 'gl', 0, 0)  12.6 us
    all_to_all x2, waiting for transfers between devices, gather(): lax.all_to_all(jnp.broadcast_to(block[None], (PARTS, *block.shape)), axis...  11 us
    all_to_all x2, starting transfers between devices, gather(): lax.all_to_all(jnp.broadcast_to(block[None], (PARTS, *block.shape)), axis...  8.99 us
  transfers between devices with their start and end apart: 2, of which 2 were waited for; matrix products, arithmetic and copies ran while one was open for 0% of the time, Pallas kernels for 8%

profile of v3, /device:TPU:64, one launch (start us, length us, event | category | flops | bytes accessed | tf_op | source)
XLA Modules:
  0.0 133.5 jit_solution(5417853605192585432)
XLA Ops:
  0.6 0.0 copy-start
  0.6 4.8 %shard_map.50 = f32[8,56,128]{2,1,0:T(8,128)} custom-call(bf16[64,64,512]{2,1,0:T(8,128)(2,1)} %tensor_in.3, bf16[512,256]{1,0:T(8,128)(2,1)} %factor_b_in.1, bf16[64,256]{1,0:T(8,128)(2,1)} %factor_c.3), custom_call_target="tpu_custom_call" | custom-call | tf_op jit(solution)/shard_map/pallas_call | solution.py:319
  5.4 11.5 %all_to_all.35 = f32[8,56,128]{2,1,0:T(8,128)S(1)} all-to-all(f32[8,56,128]{2,1,0:T(8,128)} %shard_map.50), channel_id=1, replica_groups=mesh['gh'=8,'gl'=8,'gy'=8] {'gy'}, dimensions={0} | all-to-all | bytes 458752 | tf_op jit(solution)/shard_map/all_to_all | solution.py:344
  17.0 0.7 broadcast_in_dim.8
  17.7 3.4 %all-to-all-start.1 = ((f32[8,56,128]{2,1,0:T(8,128)}), f32[8,56,128]{2,1,0:T(8,128)S(1)}, u32[]{:S(2)}, u32[]{:S(2)}) async-start(f32[8,56,128]{2,1,0:T(8,128)} %broadcast_in_dim.8), calls=%async_computation.1 | async-start | bytes 458752 | tf_op jit(solution)/shard_map/all_to_all | solution.py:348
  21.1 7.1 %all-to-all-done.1.gathered = f32[8,56,128]{2,1,0:T(8,128)S(1)} async-done(((f32[8,56,128]{2,1,0:T(8,128)}), f32[8,56,128]{2,1,0:T(8,128)S(1)}, u32[]{:S(2)}, u32[]{:S(2)}) %all-to-all-start.1) | async-done | bytes 229408 | tf_op jit(solution)/shard_map/all_to_all | solution.py:348
  28.2 0.0 copy-done
  28.2 3.7 %shard_map.51 = (f32[64,256]{1,0:T(8,128)}, f32[8,16,128]{2,1,0:T(8,128)S(1)}) custom-call(s32[1]{0:T(128)} %bitcast.where, f32[8,56,128]{2,1,0:T(8,128)S(1)} %all-to-all-done.1.gathered, bf16[64,256]{1,0:T(8,128)(2,1)S(1)} %copy-done), custom_call_target="tpu_custom_call" | custom-call | tf_op jit(solution)/shard_map/pallas_call | solution.py:319
  31.9 12.0 %all_to_all.36 = f32[8,16,128]{2,1,0:T(8,128)S(1)} all-to-all(f32[8,16,128]{2,1,0:T(8,128)S(1)} %get-tuple-element.5), channel_id=1, replica_groups=mesh['gh'=8,'gl'=8,'gy'=8] {'gl'}, dimensions={0} | all-to-all | bytes 131072 | tf_op jit(solution)/shard_map/all_to_all | solution.py:344
  43.9 24.9 %all_to_all.37.sums_in.sums = f32[8,16,128]{2,1,0:T(8,128)} all-to-all(f32[8,16,128]{2,1,0:T(8,128)S(1)} %broadcast_in_dim.9), channel_id=1, replica_groups=mesh['gh'=8,'gl'=8,'gy'=8] {'gh'}, dimensions={0} | all-to-all | bytes 131072 | tf_op jit(solution)/shard_map/all_to_all | solution.py:348
  68.8 0.0 copy-start.1
  68.8 0.0 copy-start.2
  68.8 4.7 %shard_map.52 = f32[8,72,256]{2,1,0:T(8,128)} custom-call(bf16[64,64,512]{2,1,0:T(8,128)(2,1)} %tensor_in.3, f32[64,256]{1,0:T(8,128)} %get-tuple-element.8.a_hat_in, f32[8,16,128]{2,1,0:T(8,128)} %all_to_all.37.sums_in.sums, bf16[64,256]{1,0:T(8,128)(2,1)} %factor_c.3), custom_call_target="tpu_custom_call" | custom-call | tf_op jit(solution)/shard_map/pallas_call | solution.py:319
  73.5 12.6 %all_to_all.38 = f32[8,72,256]{2,1,0:T(8,128)S(1)} all-to-all(f32[8,72,256]{2,1,0:T(8,128)} %shard_map.52), channel_id=1, replica_groups=mesh['gh'=8,'gl'=8,'gy'=8] {'gl'}, dimensions={0} | all-to-all | bytes 1179648 | tf_op jit(solution)/shard_map/all_to_all | solution.py:377
  86.1 0.8 broadcast_in_dim.10
  86.9 5.6 %all-to-all-start.5 = ((f32[8,64,256]{2,1,0:T(8,128)}), f32[8,64,256]{2,1,0:T(8,128)S(1)}, u32[]{:S(2)}, u32[]{:S(2)}) async-start(f32[8,64,256]{2,1,0:T(8,128)} %broadcast_in_dim.10), calls=%async_computation.5 | async-start | bytes 1048576 | tf_op jit(solution)/shard_map/all_to_all | solution.py:348
  92.5 12.8 %all-gather = f32[64,8,128]{2,1,0:T(8,128)S(1)} all-gather(f32[8,8,128]{2,1,0:T(8,128)S(1)} %slice.9), channel_id=2, replica_groups=mesh['gh'=8,'gl'=8,'gy'=8] {'gy'}, dimensions={0}, use_global_device_ids=true | all-gather | bytes 294912 | tf_op jit(solution)/shard_map/all_gather | solution.py:379
  105.4 0.0 copy-done.1
  105.4 0.0 copy-done.2
  105.4 10.5 %shard_map.53.inverse = f32[256,256]{1,0:T(8,128)S(1)} custom-call(f32[8,8,8,128]{3,2,1,0:T(8,128)S(1)} %bitcast.3, f32[8,16,128]{2,1,0:T(8,128)S(1)} %copy-done.2, bf16[64,256]{1,0:T(8,128)(2,1)S(1)} %copy-done.1), custom_call_target="tpu_custom_call" | custom-call | flops 12000000000 | bytes 1000000 | tf_op jit(solution)/shard_map/pallas_call | solution.py:319
  115.8 3.9 %all-to-all-done.5.m_second = f32[8,64,256]{2,1,0:T(8,128)S(1)} async-done(((f32[8,64,256]{2,1,0:T(8,128)}), f32[8,64,256]{2,1,0:T(8,128)S(1)}, u32[]{:S(2)}, u32[]{:S(2)}) %all-to-all-start.5) | async-done | bytes 524320 | tf_op jit(solution)/shard_map/all_to_all | solution.py:348
  119.8 0.3 shard_map.54
  120.1 12.6 %all_to_all.39 = f32[8,64,256]{2,1,0:T(8,128)S(1)} all-to-all(f32[8,64,256]{2,1,0:T(8,128)S(1)} %broadcast_in_dim.11), channel_id=1, replica_groups=mesh['gh'=8,'gl'=8,'gy'=8] {'gl'}, dimensions={0} | all-to-all | bytes 1048576 | tf_op jit(solution)/shard_map/all_to_all | solution.py:348
  132.7 0.8 copy.6
  (6 shorter events, 0.1 us)
Async XLA Ops:
  0.6 27.6 %copy-start = (bf16[64,256]{1,0:T(8,128)(2,1)S(1)}, bf16[64,256]{1,0:T(8,128)(2,1)}, u32[]{:S(2)}) copy-start(bf16[64,256]{1,0:T(8,128)(2,1)} %factor_c.3) | copy-start | bytes 98308
  17.7 10.5 %all-to-all-start.1 = ((f32[8,56,128]{2,1,0:T(8,128)}), f32[8,56,128]{2,1,0:T(8,128)S(1)}, u32[]{:S(2)}, u32[]{:S(2)}) async-start(f32[8,56,128]{2,1,0:T(8,128)} %broadcast_in_dim.8), calls=%async_computation.1 | async-start | bytes 458752 | tf_op jit(solution)/shard_map/all_to_all | solution.py:348
  68.8 36.6 %copy-start.1 = (bf16[64,256]{1,0:T(8,128)(2,1)S(1)}, bf16[64,256]{1,0:T(8,128)(2,1)}, u32[]{:S(2)}) copy-start(bf16[64,256]{1,0:T(8,128)(2,1)} %factor_c.3) | copy-start | bytes 98308
  68.8 36.6 %copy-start.2 = (f32[8,16,128]{2,1,0:T(8,128)S(1)}, f32[8,16,128]{2,1,0:T(8,128)}, u32[]{:S(2)}) copy-start(f32[8,16,128]{2,1,0:T(8,128)} %all_to_all.37.sums_in.sums) | copy-start | bytes 196612
  86.9 32.8 %all-to-all-start.5 = ((f32[8,64,256]{2,1,0:T(8,128)}), f32[8,64,256]{2,1,0:T(8,128)S(1)}, u32[]{:S(2)}, u32[]{:S(2)}) async-start(f32[8,64,256]{2,1,0:T(8,128)} %broadcast_in_dim.10), calls=%async_computation.5 | async-start | bytes 1048576 | tf_op jit(solution)/shard_map/all_to_all | solution.py:348

commit v4 on v3

--- a/solution.py
+++ b/solution.py
@@ -16,6 +16,8 @@
 JOINED = 2
 SLOTS = 5
 PARTS = 8
+HALVES = 2
+FAR = ("zh", "zb")
 AHEAD = 2
 STEPS = 12
 RESIDUAL = 1e-8
@@ -344,8 +346,8 @@
     return jnp.sum(lax.all_to_all(parts, axis, 0, 0), axis=0)
 
 
-def gather(block, axis):
-    return lax.all_to_all(jnp.broadcast_to(block[None], (PARTS, *block.shape)), axis, 0, 0)
+def gather(block, axis, size=PARTS):
+    return lax.all_to_all(jnp.broadcast_to(block[None], (size, *block.shape)), axis, 0, 0)
 
 
 def local(tensor, factor_b, factor_c):
@@ -370,24 +372,26 @@
         in_specs=[pl.BlockSpec(memory_space=pltpu.SMEM), whole, whole],
     )
 
-    sums = gather(scatter_sum(slab, "gl"), "gh")
+    sums = gather(scatter_sum(slab, "gl"), FAR)
     product = stream(
         second_mode_kernel, f32(PARTS, y_rows // PARTS + GROUP, rank), tensor, a_hat, sums, factor_c
     )
     received = lax.all_to_all(product, "gl", 0, 0)
-    m_second = gather(jnp.sum(received[:, : y_rows // PARTS], axis=0), "gh")
+    halves = jnp.sum(received[:, : y_rows // PARTS], axis=0).reshape(HALVES, y_rows // PARTS // HALVES, rank)
+    repeated = jnp.broadcast_to(halves[None], (PARTS // HALVES, *halves.shape)).reshape(PARTS, *halves.shape[1:])
+    m_second = lax.all_to_all(repeated, FAR, 0, 0)
     pieces = lax.all_gather(received[:, y_rows // PARTS :, :LANES], "gy")
     inverse = call(
         second_inverse_kernel, f32(rank, rank), pieces, sums, factor_c, scratch=[square], cost_estimate=INVERSE_COST
     )
-    b_band = call(second_solve_kernel, f32(y_rows // PARTS, rank), m_second, inverse)
-    b_hat = gather(b_band, "gl").reshape(y_rows, rank)
+    b_band = call(second_solve_kernel, f32(*halves.shape[1:]), m_second, inverse)
+    b_hat = gather(b_band, ("gl", "zb"), PARTS * HALVES).reshape(y_rows, rank)
     return (a_hat, b_hat)
 
 
 def solution(mesh):
-    split = Mesh(mesh.devices.reshape(PARTS, PARTS, PARTS), ("gh", "gl", "gy"))
-    x_axes = ("gh", "gl")
+    split = Mesh(mesh.devices.reshape(PARTS // HALVES, HALVES, PARTS, PARTS), ("zh", "zb", "gl", "gy"))
+    x_axes = (*FAR, "gl")
     return jax.shard_map(
         local,
         mesh=split,

time: 134 us -> 140 us (1.045)
  the two profiles are of different devices: /device:TPU:64 before, /device:TPU:8 now
where the time goes in v4:
time: 140 us; the launch traced here: 139 us
  blocking collectives  96.9 us (69%)
  Pallas kernels  25.1 us (18%)
  waiting for transfers between devices  7.11 us (5%)
  starting transfers between devices  6.82 us (5%)
  local copies, waits for them, and re-layouts  2.29 us (2%)
    all_to_all x2, blocking collectives, gather(): lax.all_to_all(jnp.broadcast_to(block[None], (size, *block.shape)), axis,...  47.8 us
    pallas_call x5, Pallas kernels, call(): pl.pallas_call(kernel, out_shape=out_shape, scratch_shapes=list(scratch),...  25.1 us
    all_to_all x2, blocking collectives, scatter_sum(): return jnp.sum(lax.all_to_all(parts, axis, 0, 0), axis=0)  23.7 us
    all_gather x1, blocking collectives, local(): pieces = lax.all_gather(received[:, y_rows // PARTS:, :LANES], 'gy')  12.8 us
    all_to_all x1, blocking collectives, local(): received = lax.all_to_all(product, 'gl', 0, 0)  12.6 us
    all_to_all x1, waiting for transfers between devices, gather(): lax.all_to_all(jnp.broadcast_to(block[None], (size, *block.shape)), axis,...  7.1 us
    all_to_all x1, starting transfers between devices, local(): m_second = lax.all_to_all(repeated, FAR, 0, 0)  3.41 us
    all_to_all x1, starting transfers between devices, gather(): lax.all_to_all(jnp.broadcast_to(block[None], (size, *block.shape)), axis,...  3.4 us
  transfers between devices with their start and end apart: 2, of which 1 were waited for; matrix products, arithmetic and copies ran while one was open for 0% of the time, Pallas kernels for 8%

profile of v4, /device:TPU:8, one launch (start us, length us, event | category | flops | bytes accessed | tf_op | source)
XLA Modules:
  0.0 139.0 jit_solution(3109564995096546219)
XLA Ops:
  0.6 0.0 copy-start
  0.6 4.8 %shard_map.50 = f32[8,56,128]{2,1,0:T(8,128)} custom-call(bf16[64,64,512]{2,1,0:T(8,128)(2,1)} %tensor_in.3, bf16[512,256]{1,0:T(8,128)(2,1)} %factor_b_in.1, bf16[64,256]{1,0:T(8,128)(2,1)} %factor_c.3), custom_call_target="tpu_custom_call" | custom-call | tf_op jit(solution)/shard_map/pallas_call | solution.py:321
  5.5 11.5 %all_to_all.35 = f32[8,56,128]{2,1,0:T(8,128)S(1)} all-to-all(f32[8,56,128]{2,1,0:T(8,128)} %shard_map.50), channel_id=1, replica_groups=mesh['zh'=4,'zb'=2,'gl'=8,'gy'=8] {'gy'}, dimensions={0} | all-to-all | bytes 458752 | tf_op jit(solution)/shard_map/all_to_all | solution.py:346
  17.0 0.7 broadcast_in_dim.10
  17.7 3.4 %all-to-all-start.1 = ((f32[8,56,128]{2,1,0:T(8,128)}), f32[8,56,128]{2,1,0:T(8,128)S(1)}, u32[]{:S(2)}, u32[]{:S(2)}) async-start(f32[8,56,128]{2,1,0:T(8,128)} %broadcast_in_dim.10), calls=%async_computation.1 | async-start | bytes 458752 | tf_op jit(solution)/shard_map/all_to_all | solution.py:350
  21.1 7.1 %all-to-all-done.1.gathered = f32[8,56,128]{2,1,0:T(8,128)S(1)} async-done(((f32[8,56,128]{2,1,0:T(8,128)}), f32[8,56,128]{2,1,0:T(8,128)S(1)}, u32[]{:S(2)}, u32[]{:S(2)}) %all-to-all-start.1) | async-done | bytes 229408 | tf_op jit(solution)/shard_map/all_to_all | solution.py:350
  28.2 0.0 copy-done
  28.2 3.7 %shard_map.51 = (f32[64,256]{1,0:T(8,128)}, f32[8,16,128]{2,1,0:T(8,128)S(1)}) custom-call(s32[1]{0:T(128)} %bitcast.where, f32[8,56,128]{2,1,0:T(8,128)S(1)} %all-to-all-done.1.gathered, bf16[64,256]{1,0:T(8,128)(2,1)S(1)} %copy-done), custom_call_target="tpu_custom_call" | custom-call | tf_op jit(solution)/shard_map/pallas_call | solution.py:321
  31.9 0.0 copy-start.1
  31.9 12.2 %all_to_all.36 = f32[8,16,128]{2,1,0:T(8,128)S(1)} all-to-all(f32[8,16,128]{2,1,0:T(8,128)S(1)} %get-tuple-element.5), channel_id=1, replica_groups=mesh['zh'=4,'zb'=2,'gl'=8,'gy'=8] {'gl'}, dimensions={0} | all-to-all | bytes 131072 | tf_op jit(solution)/shard_map/all_to_all | solution.py:346
  44.1 26.3 %all_to_all.37.sums_in.sums = f32[8,16,128]{2,1,0:T(8,128)} all-to-all(f32[8,16,128]{2,1,0:T(8,128)S(1)} %broadcast_in_dim.11), channel_id=1, replica_groups=mesh['zh'=4,'zb'=2,'gl'=8,'gy'=8] {'zh','zb'}, dimensions={0} | all-to-all | bytes 131072 | tf_op jit(solution)/shard_map/all_to_all | solution.py:350
  70.4 0.0 copy-start.2
  70.4 4.6 %shard_map.52 = f32[8,72,256]{2,1,0:T(8,128)} custom-call(bf16[64,64,512]{2,1,0:T(8,128)(2,1)} %tensor_in.3, f32[64,256]{1,0:T(8,128)} %get-tuple-element.8.a_hat_in, f32[8,16,128]{2,1,0:T(8,128)} %all_to_all.37.sums_in.sums, bf16[64,256]{1,0:T(8,128)(2,1)} %factor_c.3), custom_call_target="tpu_custom_call" | custom-call | tf_op jit(solution)/shard_map/pallas_call | solution.py:321
  75.1 12.6 %all_to_all.38 = f32[8,72,256]{2,1,0:T(8,128)S(1)} all-to-all(f32[8,72,256]{2,1,0:T(8,128)} %shard_map.52), channel_id=1, replica_groups=mesh['zh'=4,'zb'=2,'gl'=8,'gy'=8] {'gl'}, dimensions={0} | all-to-all | bytes 1179648 | tf_op jit(solution)/shard_map/all_to_all | solution.py:379
  87.7 0.7 broadcast_in_dim.13
  88.5 3.4 %all-to-all-start.5 = ((f32[8,32,256]{2,1,0:T(8,128)}), f32[8,32,256]{2,1,0:T(8,128)S(1)}, u32[]{:S(2)}, u32[]{:S(2)}) async-start(f32[8,32,256]{2,1,0:T(8,128)} %bitcast.2), calls=%async_computation.5 | async-start | bytes 524288 | tf_op jit(solution)/shard_map/all_to_all | solution.py:382
  91.9 12.8 %all-gather = f32[64,8,128]{2,1,0:T(8,128)S(1)} all-gather(f32[8,8,128]{2,1,0:T(8,128)S(1)} %slice.9), channel_id=2, replica_groups=mesh['zh'=4,'zb'=2,'gl'=8,'gy'=8] {'gy'}, dimensions={0}, use_global_device_ids=true | all-gather | bytes 294912 | tf_op jit(solution)/shard_map/all_gather | solution.py:383
  104.7 0.0 copy-done.1
  104.7 0.0 copy-done.2
  104.8 11.7 %shard_map.53.inverse = f32[256,256]{1,0:T(8,128)S(1)} custom-call(f32[8,8,8,128]{3,2,1,0:T(8,128)S(1)} %bitcast.5, f32[8,16,128]{2,1,0:T(8,128)S(1)} %copy-done.2, bf16[64,256]{1,0:T(8,128)(2,1)S(1)} %copy-done.1), custom_call_target="tpu_custom_call" | custom-call | flops 12000000000 | bytes 1000000 | tf_op jit(solution)/shard_map/pallas_call | solution.py:321
  116.5 0.0 all-to-all-done.5.m_second
  116.5 0.2 shard_map.54
  116.8 21.4 %all_to_all.39 = f32[16,32,256]{2,1,0:T(8,128)S(1)} all-to-all(f32[16,32,256]{2,1,0:T(8,128)S(1)} %broadcast_in_dim.14), channel_id=1, replica_groups=mesh['zh'=4,'zb'=2,'gl'=8,'gy'=8] {'gl','zb'}, dimensions={0} | all-to-all | bytes 1048576 | tf_op jit(solution)/shard_map/all_to_all | solution.py:350
  138.2 0.8 copy.6
  (6 shorter events, 0.1 us)
Async XLA Ops:
  0.6 27.6 %copy-start = (bf16[64,256]{1,0:T(8,128)(2,1)S(1)}, bf16[64,256]{1,0:T(8,128)(2,1)}, u32[]{:S(2)}) copy-start(bf16[64,256]{1,0:T(8,128)(2,1)} %factor_c.3) | copy-start | bytes 98308
  17.7 10.5 %all-to-all-start.1 = ((f32[8,56,128]{2,1,0:T(8,128)}), f32[8,56,128]{2,1,0:T(8,128)S(1)}, u32[]{:S(2)}, u32[]{:S(2)}) async-start(f32[8,56,128]{2,1,0:T(8,128)} %broadcast_in_dim.10), calls=%async_computation.1 | async-start | bytes 458752 | tf_op jit(solution)/shard_map/all_to_all | solution.py:350
  31.9 72.9 %copy-start.1 = (bf16[64,256]{1,0:T(8,128)(2,1)S(1)}, bf16[64,256]{1,0:T(8,128)(2,1)}, u32[]{:S(2)}) copy-start(bf16[64,256]{1,0:T(8,128)(2,1)} %factor_c.3) | copy-start | bytes 98308
  70.4 34.3 %copy-start.2 = (f32[8,16,128]{2,1,0:T(8,128)S(1)}, f32[8,16,128]{2,1,0:T(8,128)}, u32[]{:S(2)}) copy-start(f32[8,16,128]{2,1,0:T(8,128)} %all_to_all.37.sums_in.sums) | copy-start | bytes 196612
  88.5 28.0 %all-to-all-start.5 = ((f32[8,32,256]{2,1,0:T(8,128)}), f32[8,32,256]{2,1,0:T(8,128)S(1)}, u32[]{:S(2)}, u32[]{:S(2)}) async-start(f32[8,32,256]{2,1,0:T(8,128)} %bitcast.2), calls=%async_computation.5 | async-start | bytes 524288 | tf_op jit(solution)/shard_map/all_to_all | solution.py:382

commit v5 on v4

--- a/solution.py
+++ b/solution.py
@@ -17,6 +17,8 @@
 SLOTS = 5
 PARTS = 8
 HALVES = 2
+GY = ("x", "core")
+CORES = 2
 FAR = ("zh", "zb")
 AHEAD = 2
 STEPS = 12
@@ -207,16 +209,20 @@
     return half + jnp.where(row_block == col_block, 0.0, half).T
 
 
-def first_mode_kernel(tensor_in, factor_b_in, factor_c_in, out, tensor, factor_b, factor_c, arrived, arrived_small):
+def first_mode_kernel(
+    core, tensor_in, factor_b_in, factor_c_in, out, tensor, factor_b, factor_c, arrived, arrived_small
+):
     x_rows, time_len, depth = tensor.shape
     rank = factor_b.shape[1]
     rows = x_rows // PARTS
     wait_part = fetch(
         tensor_in, tensor, [factor_b_in, factor_c_in], [factor_b, factor_c], arrived, arrived_small
     )
+    half = PARTS // CORES
     for t, slot in enumerate(packed_gram(bf16_gram(factor_b[...]))):
         for i in range(PARTS):
-            out[i, t * GROUP : (t + 1) * GROUP, :] = slot[i * GROUP : (i + 1) * GROUP]
+            side = core[0] if i < half else 1 - core[0]
+            out[side, i % half, t * GROUP : (t + 1) * GROUP, :] = slot[i * GROUP : (i + 1) * GROUP]
 
     def contract(i, carry):
         wait_part(i)
@@ -227,17 +233,21 @@
         ).reshape(rows, time_len, rank)
         summed = jnp.sum(contracted * factor_c[...].astype(jnp.float32)[None], axis=1)
         for h in range(rank // LANES):
-            out[i, pl.ds((SLOTS + h) * GROUP, rows), :] = summed[:, h * LANES : (h + 1) * LANES]
+            side, place = jnp.where(i < half, core[0], 1 - core[0]), jnp.where(i < half, i, i - half)
+            out[side, place, pl.ds((SLOTS + h) * GROUP, rows), :] = summed[:, h * LANES : (h + 1) * LANES]
         return carry
 
     lax.fori_loop(0, PARTS, contract, 0)
 
 
-def first_solve_kernel(where, gathered, factor_c, a_hat, slab, work, inverse, raw):
+def first_solve_kernel(where, mine, other, factor_c, a_hat, slab, work, inverse, raw):
     rank = work.shape[0]
     share = rank // PARTS
+    half = PARTS // CORES
+    core = where[0] % CORES
+    gathered = [jnp.where(core == p // half, mine[p % half], other[p % half]) for p in range(PARTS)]
     bands = [
-        jnp.concatenate([gathered[p, t * GROUP : (t + 1) * GROUP, :] for p in range(PARTS)], axis=0)
+        jnp.concatenate([gathered[p][t * GROUP : (t + 1) * GROUP] for p in range(PARTS)], axis=0)
         for t in range(SLOTS + rank // LANES)
     ]
     b_gram = unpacked_gram(bands[:SLOTS])
@@ -327,10 +337,11 @@
     )(*operands)
 
 
-def stream(kernel, out_shape, *operands):
+def stream(kernel, out_shape, *operands, scalars=()):
     return call(
         kernel,
         out_shape,
+        *scalars,
         *operands,
         scratch=[
             *(pltpu.VMEM(x.shape, x.dtype) for x in operands),
@@ -338,8 +349,13 @@
             pltpu.SemaphoreType.DMA((len(operands) - 1,)),
         ],
         vmem=STREAM_BYTES,
-        in_specs=[pl.BlockSpec(memory_space=pl.ANY)] * len(operands),
-    )
+        in_specs=[pl.BlockSpec(memory_space=pltpu.SMEM)] * len(scalars)
+        + [pl.BlockSpec(memory_space=pl.ANY)] * len(operands),
+    )
+
+
+def swap_cores(value):
+    return lax.ppermute(value, "core", [(0, 1), (1, 0)])
 
 
 def scatter_sum(parts, axis):
@@ -356,20 +372,29 @@
     square = pltpu.VMEM((rank, rank), jnp.float32)
 
     whole = pl.BlockSpec(memory_space=pltpu.VMEM)
+    where = lax.axis_index(GY).astype(jnp.int32).reshape(1)
+    core = lax.axis_index("core").astype(jnp.int32).reshape(1)
     first = stream(
-        first_mode_kernel, f32(PARTS, (SLOTS + rank // LANES) * GROUP, LANES), tensor, factor_b, factor_c
-    )
-    gathered = gather(scatter_sum(first, "gy"), "gy")
-
-    where = lax.axis_index("gy").astype(jnp.int32).reshape(1)
+        first_mode_kernel,
+        f32(CORES, PARTS // CORES, (SLOTS + rank // LANES) * GROUP, LANES),
+        tensor,
+        factor_b,
+        factor_c,
+        scalars=[core],
+    )
+    pair = first[0] + swap_cores(first[1])
+    mine = jnp.sum(gather(pair, "x", PARTS // CORES), axis=0)
+    other = swap_cores(mine)
+
     a_hat, slab = call(
         first_solve_kernel,
         (f32(x_rows, rank), f32(PARTS, 2 * GROUP, LANES)),
         where,
-        gathered,
+        mine,
+        other,
         factor_c,
         scratch=[square, square, square],
-        in_specs=[pl.BlockSpec(memory_space=pltpu.SMEM), whole, whole],
+        in_specs=[pl.BlockSpec(memory_space=pltpu.SMEM), whole, whole, whole],
     )
 
     sums = gather(scatter_sum(slab, "gl"), FAR)
@@ -380,7 +405,7 @@
     halves = jnp.sum(received[:, : y_rows // PARTS], axis=0).reshape(HALVES, y_rows // PARTS // HALVES, rank)
     repeated = jnp.broadcast_to(halves[None], (PARTS // HALVES, *halves.shape)).reshape(PARTS, *halves.shape[1:])
     m_second = lax.all_to_all(repeated, FAR, 0, 0)
-    pieces = lax.all_gather(received[:, y_rows // PARTS :, :LANES], "gy")
+    pieces = lax.all_gather(received[:, y_rows // PARTS :, :LANES], GY)
     inverse = call(
         second_inverse_kernel, f32(rank, rank), pieces, sums, factor_c, scratch=[square], cost_estimate=INVERSE_COST
     )
@@ -390,12 +415,13 @@
 
 
 def solution(mesh):
-    split = Mesh(mesh.devices.reshape(PARTS // HALVES, HALVES, PARTS, PARTS), ("zh", "zb", "gl", "gy"))
+    z_and_y = (PARTS // HALVES, HALVES, PARTS)
+    split = Mesh(mesh.devices.reshape(*z_and_y, PARTS // CORES, CORES), (*FAR, "gl", *GY))
     x_axes = (*FAR, "gl")
     return jax.shard_map(
         local,
         mesh=split,
-        in_specs=(P(x_axes, None, "gy"), P("gy", None), P()),
-        out_specs=(P(x_axes, None), P("gy", None)),
+        in_specs=(P(x_axes, None, GY), P(GY, None), P()),
+        out_specs=(P(x_axes, None), P(GY, None)),
         check_vma=False,
     )

time: 140 us -> 137 us (0.979)
  waiting for transfers between devices: 7.11 us -> 2.58 us
  blocking collectives: 96.9 us -> 98.6 us
    all_to_all x2 -> x3, blocking collectives: 47.8 us -> 61.3 us  [gather(): lax.all_to_all(jnp.broadcast_to(block[None], (size, *block.shape)), axis,...]
    all_to_all x2 -> x1, blocking collectives: 23.7 us -> 11.8 us  [scatter_sum(): return jnp.sum(lax.all_to_all(parts, axis, 0, 0), axis=0)]
    all_to_all x1 -> x0, waiting for transfers between devices: 7.1 us -> none  [gather(): lax.all_to_all(jnp.broadcast_to(block[None], (size, *block.shape)), axis,...]
    ppermute x0 -> x2, starting transfers between devices: none -> 3.83 us  [swap_cores(): return lax.ppermute(value, 'core', [(0, 1), (1, 0)])]
    all_to_all x1 -> x0, starting transfers between devices: 3.4 us -> none  [gather(): lax.all_to_all(jnp.broadcast_to(block[None], (size, *block.shape)), axis,...]
    ppermute x0 -> x2, waiting for transfers between devices: none -> 2.57 us  [swap_cores(): return lax.ppermute(value, 'core', [(0, 1), (1, 0)])]
  transfers between devices with their start and end apart: 2 -> 3, of which waited for: 1 -> 2; matrix products, arithmetic and copies ran while one was open for 0% -> 0% of each run, Pallas kernels for 8% -> 8%
where the time goes in v5:
time: 137 us
  blocking collectives  98.6 us (72%)
  Pallas kernels  24 us (18%)
  starting transfers between devices  7.24 us (5%)
  waiting for transfers between devices  2.58 us (2%)
  local copies, waits for them, and re-layouts  2.53 us (2%)
    all_to_all x3, blocking collectives, gather(): lax.all_to_all(jnp.broadcast_to(block[None], (size, *block.shape)), axis,...  61.3 us
    pallas_call x5, Pallas kernels, call(): pl.pallas_call(kernel, out_shape=out_shape, scratch_shapes=list(scratch),...  24 us
    all_gather x1, blocking collectives, local(): pieces = lax.all_gather(received[:, y_rows // PARTS:, :LANES], GY)  12.8 us
    all_to_all x1, blocking collectives, local(): received = lax.all_to_all(product, 'gl', 0, 0)  12.6 us
    all_to_all x1, blocking collectives, scatter_sum(): return jnp.sum(lax.all_to_all(parts, axis, 0, 0), axis=0)  11.8 us
    ppermute x2, starting transfers between devices, swap_cores(): return lax.ppermute(value, 'core', [(0, 1), (1, 0)])  3.83 us
    all_to_all x1, starting transfers between devices, local(): m_second = lax.all_to_all(repeated, FAR, 0, 0)  3.41 us
  transfers between devices with their start and end apart: 3, of which 2 were waited for; matrix products, arithmetic and copies ran while one was open for 0% of the time, Pallas kernels for 8%

profile of v5, /device:TPU:8, one launch (start us, length us, event | category | flops | bytes accessed | tf_op | source)
XLA Modules:
  0.0 136.7 jit_solution(11356151857607559858)
XLA Ops:
  0.6 0.0 copy-start
  0.6 4.8 %shard_map.50 = f32[2,4,56,128]{3,2,1,0:T(8,128)} custom-call(s32[1]{0:T(128)} %bitcast.1.core, bf16[64,64,512]{2,1,0:T(8,128)(2,1)} %tensor_in.3, bf16[512,256]{1,0:T(8,128)(2,1)} %factor_b_in.1, bf16[64,256]{1,0:T(8,128)(2,1)} %factor_c.3), custom_call_target="tpu_custom_call" | custom-call | tf_op jit(solution)/shard_map/pallas_call | solution.py:331
  5.5 0.9 slice_bitcast_fusion
  6.4 1.9 %collective-permute-start = (f32[4,56,128]{2,1,0:T(8,128)S(1)}, f32[4,56,128]{2,1,0:T(8,128)S(1)}, u32[]{:S(2)}, u32[]{:S(2)}) collective-permute-start(f32[4,56,128]{2,1,0:T(8,128)S(1)} %slice_bitcast_fusion), channel_id=1, source_target_pairs={{0,1},{1,0},{2,3},{3,2},{4,5},{5,4},{6,7},{7,6},{8,9},{9,8},{10,11... | collective-permute-start | bytes 344072 | tf_op jit(solution)/shard_map/ppermute | solution.py:358
  8.3 1.3 collective-permute-done
  9.6 0.9 fusion
  10.5 13.2 %all_to_all.30 = f32[4,4,56,128]{3,2,1,0:T(8,128)S(1)} all-to-all(f32[4,4,56,128]{3,2,1,0:T(8,128)S(1)} %broadcast_in_dim.10), channel_id=1, replica_groups=mesh['zh'=4,'zb'=2,'gl'=8,'x'=4,'core'=2] {'x'}, dimensions={0} | all-to-all | bytes 917504 | tf_op jit(solution)/shard_map/all_to_all | solution.py:366
  23.7 1.9 %collective-permute-start.1 = (f32[4,56,128]{2,1,0:T(8,128)S(1)}, f32[4,56,128]{2,1,0:T(8,128)S(1)}, u32[]{:S(2)}, u32[]{:S(2)}) collective-permute-start(f32[4,56,128]{2,1,0:T(8,128)S(1)} %reduce_sum.27.mine), channel_id=1, source_target_pairs={{0,1},{1,0},{2,3},{3,2},{4,5},{5,4},{6,7},{7,6},{8,9},{9,8},{10,11... | collective-permute-start | bytes 344072 | tf_op jit(solution)/shard_map/ppermute | solution.py:358
  25.7 1.3 collective-permute-done.1.other
  26.9 0.0 copy-done
  27.0 3.7 %shard_map.51 = (f32[64,256]{1,0:T(8,128)}, f32[8,16,128]{2,1,0:T(8,128)S(1)}) custom-call(s32[1]{0:T(128)} %bitcast.where, f32[4,56,128]{2,1,0:T(8,128)S(1)} %reduce_sum.27.mine, f32[4,56,128]{2,1,0:T(8,128)S(1)} %collective-permute-done.1.other, bf16[64,256]{1,0:T(8,128)(2,1)S(1)} %copy-done), custom_call_target="tpu_custom_call" | custom-call | tf_op jit(solution)/shard_map/pallas_call | solution.py:331
  30.6 11.8 %all_to_all.31 = f32[8,16,128]{2,1,0:T(8,128)S(1)} all-to-all(f32[8,16,128]{2,1,0:T(8,128)S(1)} %get-tuple-element.5), channel_id=1, replica_groups=mesh['zh'=4,'zb'=2,'gl'=8,'x'=4,'core'=2] {'gl'}, dimensions={0} | all-to-all | bytes 131072 | tf_op jit(solution)/shard_map/all_to_all | solution.py:362
  42.5 26.7 %all_to_all.32.sums_in.sums = f32[8,16,128]{2,1,0:T(8,128)} all-to-all(f32[8,16,128]{2,1,0:T(8,128)S(1)} %broadcast_in_dim.11), channel_id=1, replica_groups=mesh['zh'=4,'zb'=2,'gl'=8,'x'=4,'core'=2] {'zh','zb'}, dimensions={0} | all-to-all | bytes 131072 | tf_op jit(solution)/shard_map/all_to_all | solution.py:366
  69.2 4.6 %shard_map.52 = f32[8,72,256]{2,1,0:T(8,128)} custom-call(bf16[64,64,512]{2,1,0:T(8,128)(2,1)} %tensor_in.3, f32[64,256]{1,0:T(8,128)} %get-tuple-element.8.a_hat_in, f32[8,16,128]{2,1,0:T(8,128)} %all_to_all.32.sums_in.sums, bf16[64,256]{1,0:T(8,128)(2,1)} %factor_c.3), custom_call_target="tpu_custom_call" | custom-call | tf_op jit(solution)/shard_map/pallas_call | solution.py:331
  73.8 12.6 %all_to_all.33 = f32[8,72,256]{2,1,0:T(8,128)S(1)} all-to-all(f32[8,72,256]{2,1,0:T(8,128)} %shard_map.52), channel_id=1, replica_groups=mesh['zh'=4,'zb'=2,'gl'=8,'x'=4,'core'=2] {'gl'}, dimensions={0} | all-to-all | bytes 1179648 | tf_op jit(solution)/shard_map/all_to_all | solution.py:404
  86.5 0.7 broadcast_in_dim.13
  87.2 3.4 %all-to-all-start.4 = ((f32[8,32,256]{2,1,0:T(8,128)}), f32[8,32,256]{2,1,0:T(8,128)S(1)}, u32[]{:S(2)}, u32[]{:S(2)}) async-start(f32[8,32,256]{2,1,0:T(8,128)} %bitcast.5), calls=%async_computation.4 | async-start | bytes 524288 | tf_op jit(solution)/shard_map/all_to_all | solution.py:407
  90.7 12.8 %all-gather = f32[64,8,128]{2,1,0:T(8,128)S(1)} all-gather(f32[8,8,128]{2,1,0:T(8,128)S(1)} %slice.19), channel_id=2, replica_groups=mesh['zh'=4,'zb'=2,'gl'=8,'x'=4,'core'=2] {'x','core'}, dimensions={0}, use_global_device_ids=true | all-gather | bytes 294912 | tf_op jit(solution)/shard_map/all_gather | solution.py:408
  103.5 0.0 copy-done.1
  103.5 10.6 %shard_map.53.inverse = f32[256,256]{1,0:T(8,128)S(1)} custom-call(f32[8,8,8,128]{3,2,1,0:T(8,128)S(1)} %bitcast.12, f32[8,16,128]{2,1,0:T(8,128)S(1)} %copy-done.2, bf16[64,256]{1,0:T(8,128)(2,1)S(1)} %copy-done.1), custom_call_target="tpu_custom_call" | custom-call | flops 12000000000 | bytes 1000000 | tf_op jit(solution)/shard_map/pallas_call | solution.py:331
  114.1 0.0 all-to-all-done.4.m_second
  114.2 0.2 shard_map.54
  114.5 21.4 %all_to_all.34 = f32[16,32,256]{2,1,0:T(8,128)S(1)} all-to-all(f32[16,32,256]{2,1,0:T(8,128)S(1)} %broadcast_in_dim.14), channel_id=1, replica_groups=mesh['zh'=4,'zb'=2,'gl'=8,'x'=4,'core'=2] {'gl','zb'}, dimensions={0} | all-to-all | bytes 1048576 | tf_op jit(solution)/shard_map/all_to_all | solution.py:366
  135.9 0.8 copy.6
  (10 shorter events, 0.2 us)
Async XLA Ops:
  0.6 26.3 %copy-start = (bf16[64,256]{1,0:T(8,128)(2,1)S(1)}, bf16[64,256]{1,0:T(8,128)(2,1)}, u32[]{:S(2)}) copy-start(bf16[64,256]{1,0:T(8,128)(2,1)} %factor_c.3) | copy-start | bytes 98308
  6.4 3.2 %collective-permute-start = (f32[4,56,128]{2,1,0:T(8,128)S(1)}, f32[4,56,128]{2,1,0:T(8,128)S(1)}, u32[]{:S(2)}, u32[]{:S(2)}) collective-permute-start(f32[4,56,128]{2,1,0:T(8,128)S(1)} %slice_bitcast_fusion), channel_id=1, source_target_pairs={{0,1},{1,0},{2,3},{3,2},{4,5},{5,4},{6,7},{7,6},{8,9},{9,8},{10,11... | collective-permute-start | bytes 344072 | tf_op jit(solution)/shard_map/ppermute | solution.py:358
  23.7 3.2 %collective-permute-start.1 = (f32[4,56,128]{2,1,0:T(8,128)S(1)}, f32[4,56,128]{2,1,0:T(8,128)S(1)}, u32[]{:S(2)}, u32[]{:S(2)}) collective-permute-start(f32[4,56,128]{2,1,0:T(8,128)S(1)} %reduce_sum.27.mine), channel_id=1, source_target_pairs={{0,1},{1,0},{2,3},{3,2},{4,5},{5,4},{6,7},{7,6},{8,9},{9,8},{10,11... | collective-permute-start | bytes 344072 | tf_op jit(solution)/shard_map/ppermute | solution.py:358
  30.6 72.9 %copy-start.1 = (bf16[64,256]{1,0:T(8,128)(2,1)S(1)}, bf16[64,256]{1,0:T(8,128)(2,1)}, u32[]{:S(2)}) copy-start(bf16[64,256]{1,0:T(8,128)(2,1)} %factor_c.3) | copy-start | bytes 98308
  69.2 34.3 %copy-start.2 = (f32[8,16,128]{2,1,0:T(8,128)S(1)}, f32[8,16,128]{2,1,0:T(8,128)}, u32[]{:S(2)}) copy-start(f32[8,16,128]{2,1,0:T(8,128)} %all_to_all.32.sums_in.sums) | copy-start | bytes 196612
  87.2 26.9 %all-to-all-start.4 = ((f32[8,32,256]{2,1,0:T(8,128)}), f32[8,32,256]{2,1,0:T(8,128)S(1)}, u32[]{:S(2)}, u32[]{:S(2)}) async-start(f32[8,32,256]{2,1,0:T(8,128)} %bitcast.5), calls=%async_computation.4 | async-start | bytes 524288 | tf_op jit(solution)/shard_map/all_to_all | solution.py:407

commit v6 on v5

--- a/solution.py
+++ b/solution.py
@@ -210,7 +210,7 @@
 
 
 def first_mode_kernel(
-    core, tensor_in, factor_b_in, factor_c_in, out, tensor, factor_b, factor_c, arrived, arrived_small
+    core, tensor_in, factor_b_in, factor_c_in, keep, give, tensor, factor_b, factor_c, arrived, arrived_small, out
 ):
     x_rows, time_len, depth = tensor.shape
     rank = factor_b.shape[1]
@@ -221,8 +221,7 @@
     half = PARTS // CORES
     for t, slot in enumerate(packed_gram(bf16_gram(factor_b[...]))):
         for i in range(PARTS):
-            side = core[0] if i < half else 1 - core[0]
-            out[side, i % half, t * GROUP : (t + 1) * GROUP, :] = slot[i * GROUP : (i + 1) * GROUP]
+            out[i // half, i % half, t * GROUP : (t + 1) * GROUP, :] = slot[i * GROUP : (i + 1) * GROUP]
 
     def contract(i, carry):
         wait_part(i)
@@ -233,11 +232,13 @@
         ).reshape(rows, time_len, rank)
         summed = jnp.sum(contracted * factor_c[...].astype(jnp.float32)[None], axis=1)
         for h in range(rank // LANES):
-            side, place = jnp.where(i < half, core[0], 1 - core[0]), jnp.where(i < half, i, i - half)
-            out[side, place, pl.ds((SLOTS + h) * GROUP, rows), :] = summed[:, h * LANES : (h + 1) * LANES]
+            out[i // half, i % half, pl.ds((SLOTS + h) * GROUP, rows), :] = summed[:, h * LANES : (h + 1) * LANES]
         return carry
 
     lax.fori_loop(0, PARTS, contract, 0)
+    first = core[0] == 0
+    keep[...] = jnp.where(first, out[0], out[1])
+    give[...] = jnp.where(first, out[1], out[0])
 
 
 def first_solve_kernel(where, mine, other, factor_c, a_hat, slab, work, inverse, raw):
@@ -337,7 +338,7 @@
     )(*operands)
 
 
-def stream(kernel, out_shape, *operands, scalars=()):
+def stream(kernel, out_shape, *operands, scalars=(), scratch=()):
     return call(
         kernel,
         out_shape,
@@ -347,6 +348,7 @@
             *(pltpu.VMEM(x.shape, x.dtype) for x in operands),
             pltpu.SemaphoreType.DMA((PARTS,)),
             pltpu.SemaphoreType.DMA((len(operands) - 1,)),
+            *scratch,
         ],
         vmem=STREAM_BYTES,
         in_specs=[pl.BlockSpec(memory_space=pltpu.SMEM)] * len(scalars)
@@ -374,15 +376,17 @@
     whole = pl.BlockSpec(memory_space=pltpu.VMEM)
     where = lax.axis_index(GY).astype(jnp.int32).reshape(1)
     core = lax.axis_index("core").astype(jnp.int32).reshape(1)
-    first = stream(
+    half = f32(PARTS // CORES, (SLOTS + rank // LANES) * GROUP, LANES)
+    keep, give = stream(
         first_mode_kernel,
-        f32(CORES, PARTS // CORES, (SLOTS + rank // LANES) * GROUP, LANES),
+        (half, half),
         tensor,
         factor_b,
         factor_c,
         scalars=[core],
-    )
-    pair = first[0] + swap_cores(first[1])
+        scratch=[pltpu.VMEM((CORES, *half.shape), jnp.float32)],
+    )
+    pair = keep + swap_cores(give)
     mine = jnp.sum(gather(pair, "x", PARTS // CORES), axis=0)
     other = swap_cores(mine)
 

time: 137 us -> 137 us (level)
  no operation moved by 1% of the time
where the time goes in v6:
time: 137 us; the launch traced here: 136 us
  blocking collectives  98.6 us (72%)
  Pallas kernels  24 us (18%)
  starting transfers between devices  7.25 us (5%)
  waiting for transfers between devices  2.79 us (2%)
  local copies, waits for them, and re-layouts  1.62 us (1%)
    all_to_all x3, blocking collectives, gather(): lax.all_to_all(jnp.broadcast_to(block[None], (size, *block.shape)), axis,...  61.4 us
    pallas_call x5, Pallas kernels, call(): pl.pallas_call(kernel, out_shape=out_shape, scratch_shapes=list(scratch),...  24 us
    all_gather x1, blocking collectives, local(): pieces = lax.all_gather(received[:, y_rows // PARTS:, :LANES], GY)  12.8 us
    all_to_all x1, blocking collectives, local(): received = lax.all_to_all(product, 'gl', 0, 0)  12.6 us
    all_to_all x1, blocking collectives, scatter_sum(): return jnp.sum(lax.all_to_all(parts, axis, 0, 0), axis=0)  11.8 us
    ppermute x2, starting transfers between devices, swap_cores(): return lax.ppermute(value, 'core', [(0, 1), (1, 0)])  3.84 us
    all_to_all x1, starting transfers between devices, local(): m_second = lax.all_to_all(repeated, FAR, 0, 0)  3.41 us
    ppermute x2, waiting for transfers between devices, swap_cores(): return lax.ppermute(value, 'core', [(0, 1), (1, 0)])  2.78 us
  transfers between devices with their start and end apart: 3, of which 2 were waited for; matrix products, arithmetic and copies ran while one was open for 0% of the time, Pallas kernels for 8%

profile of v6, /device:TPU:8, one launch (start us, length us, event | category | flops | bytes accessed | tf_op | source)
XLA Modules:
  0.0 136.0 jit_solution(1137170070436257227)
XLA Ops:
  0.6 0.0 copy-start
  0.6 4.8 %shard_map.50 = (f32[4,56,128]{2,1,0:T(8,128)}, f32[4,56,128]{2,1,0:T(8,128)}) custom-call(s32[1]{0:T(128)} %bitcast.1.core, bf16[64,64,512]{2,1,0:T(8,128)(2,1)} %tensor_in.3, bf16[512,256]{1,0:T(8,128)(2,1)} %factor_b_in.1, bf16[64,256]{1,0:T(8,128)(2,1)} %factor_c.3), custom_call_target="tpu_custom_call" | custom-call | tf_op jit(solution)/shard_map/pallas_call | solution.py:332
  5.4 1.9 %collective-permute-start = (f32[4,56,128]{2,1,0:T(8,128)}, f32[4,56,128]{2,1,0:T(8,128)S(1)}, u32[]{:S(2)}, u32[]{:S(2)}) collective-permute-start(f32[4,56,128]{2,1,0:T(8,128)} %get-tuple-element.7), channel_id=1, source_target_pairs={{0,1},{1,0},{2,3},{3,2},{4,5},{5,4},{6,7},{7,6},{8,9},{9,8},{10,11... | collective-permute-start | bytes 344072 | tf_op jit(solution)/shard_map/ppermute | solution.py:360
  7.4 1.5 %collective-permute-done = f32[4,56,128]{2,1,0:T(8,128)S(1)} collective-permute-done((f32[4,56,128]{2,1,0:T(8,128)}, f32[4,56,128]{2,1,0:T(8,128)S(1)}, u32[]{:S(2)}, u32[]{:S(2)}) %collective-permute-start) | collective-permute-done | bytes 114720 | tf_op jit(solution)/shard_map/ppermute | solution.py:360
  8.9 0.9 add.7
  9.8 13.2 %all_to_all.30 = f32[4,4,56,128]{3,2,1,0:T(8,128)S(1)} all-to-all(f32[4,4,56,128]{3,2,1,0:T(8,128)S(1)} %broadcast_in_dim.10), channel_id=1, replica_groups=mesh['zh'=4,'zb'=2,'gl'=8,'x'=4,'core'=2] {'x'}, dimensions={0} | all-to-all | bytes 917504 | tf_op jit(solution)/shard_map/all_to_all | solution.py:368
  23.1 1.9 %collective-permute-start.1 = (f32[4,56,128]{2,1,0:T(8,128)S(1)}, f32[4,56,128]{2,1,0:T(8,128)S(1)}, u32[]{:S(2)}, u32[]{:S(2)}) collective-permute-start(f32[4,56,128]{2,1,0:T(8,128)S(1)} %reduce_sum.27.mine), channel_id=1, source_target_pairs={{0,1},{1,0},{2,3},{3,2},{4,5},{5,4},{6,7},{7,6},{8,9},{9,8},{10,11... | collective-permute-start | bytes 344072 | tf_op jit(solution)/shard_map/ppermute | solution.py:360
  25.0 1.3 collective-permute-done.1.other
  26.3 0.0 copy-done
  26.3 3.7 %shard_map.51 = (f32[64,256]{1,0:T(8,128)}, f32[8,16,128]{2,1,0:T(8,128)S(1)}) custom-call(s32[1]{0:T(128)} %bitcast.where, f32[4,56,128]{2,1,0:T(8,128)S(1)} %reduce_sum.27.mine, f32[4,56,128]{2,1,0:T(8,128)S(1)} %collective-permute-done.1.other, bf16[64,256]{1,0:T(8,128)(2,1)S(1)} %copy-done), custom_call_target="tpu_custom_call" | custom-call | tf_op jit(solution)/shard_map/pallas_call | solution.py:332
  30.0 11.8 %all_to_all.31 = f32[8,16,128]{2,1,0:T(8,128)S(1)} all-to-all(f32[8,16,128]{2,1,0:T(8,128)S(1)} %get-tuple-element.9), channel_id=1, replica_groups=mesh['zh'=4,'zb'=2,'gl'=8,'x'=4,'core'=2] {'gl'}, dimensions={0} | all-to-all | bytes 131072 | tf_op jit(solution)/shard_map/all_to_all | solution.py:364
  41.8 26.7 %all_to_all.32.sums_in.sums = f32[8,16,128]{2,1,0:T(8,128)} all-to-all(f32[8,16,128]{2,1,0:T(8,128)S(1)} %broadcast_in_dim.11), channel_id=1, replica_groups=mesh['zh'=4,'zb'=2,'gl'=8,'x'=4,'core'=2] {'zh','zb'}, dimensions={0} | all-to-all | bytes 131072 | tf_op jit(solution)/shard_map/all_to_all | solution.py:368
  68.5 4.7 %shard_map.52 = f32[8,72,256]{2,1,0:T(8,128)} custom-call(bf16[64,64,512]{2,1,0:T(8,128)(2,1)} %tensor_in.3, f32[64,256]{1,0:T(8,128)} %get-tuple-element.12.a_hat_in, f32[8,16,128]{2,1,0:T(8,128)} %all_to_all.32.sums_in.sums, bf16[64,256]{1,0:T(8,128)(2,1)} %factor_c.3), custom_call_target="tpu_custom_call" | custom-call | tf_op jit(solution)/shard_map/pallas_call | solution.py:332
  73.2 12.6 %all_to_all.33 = f32[8,72,256]{2,1,0:T(8,128)S(1)} all-to-all(f32[8,72,256]{2,1,0:T(8,128)} %shard_map.52), channel_id=1, replica_groups=mesh['zh'=4,'zb'=2,'gl'=8,'x'=4,'core'=2] {'gl'}, dimensions={0} | all-to-all | bytes 1179648 | tf_op jit(solution)/shard_map/all_to_all | solution.py:408
  85.8 0.7 broadcast_in_dim.13
  86.5 3.4 %all-to-all-start.4 = ((f32[8,32,256]{2,1,0:T(8,128)}), f32[8,32,256]{2,1,0:T(8,128)S(1)}, u32[]{:S(2)}, u32[]{:S(2)}) async-start(f32[8,32,256]{2,1,0:T(8,128)} %bitcast.3), calls=%async_computation.4 | async-start | bytes 524288 | tf_op jit(solution)/shard_map/all_to_all | solution.py:411
  90.0 12.8 %all-gather = f32[64,8,128]{2,1,0:T(8,128)S(1)} all-gather(f32[8,8,128]{2,1,0:T(8,128)S(1)} %slice.9), channel_id=2, replica_groups=mesh['zh'=4,'zb'=2,'gl'=8,'x'=4,'core'=2] {'x','core'}, dimensions={0}, use_global_device_ids=true | all-gather | bytes 294912 | tf_op jit(solution)/shard_map/all_gather | solution.py:412
  102.8 0.0 copy-done.1
  102.8 0.0 copy-done.2
  102.8 10.6 %shard_map.53.inverse = f32[256,256]{1,0:T(8,128)S(1)} custom-call(f32[8,8,8,128]{3,2,1,0:T(8,128)S(1)} %bitcast.6, f32[8,16,128]{2,1,0:T(8,128)S(1)} %copy-done.2, bf16[64,256]{1,0:T(8,128)(2,1)S(1)} %copy-done.1), custom_call_target="tpu_custom_call" | custom-call | flops 12000000000 | bytes 1000000 | tf_op jit(solution)/shard_map/pallas_call | solution.py:332
  113.5 0.0 all-to-all-done.4.m_second
  113.5 0.2 shard_map.54
  113.8 21.4 %all_to_all.34 = f32[16,32,256]{2,1,0:T(8,128)S(1)} all-to-all(f32[16,32,256]{2,1,0:T(8,128)S(1)} %broadcast_in_dim.14), channel_id=1, replica_groups=mesh['zh'=4,'zb'=2,'gl'=8,'x'=4,'core'=2] {'gl','zb'}, dimensions={0} | all-to-all | bytes 1048576 | tf_op jit(solution)/shard_map/all_to_all | solution.py:368
  135.2 0.8 copy.6
  (9 shorter events, 0.2 us)
Async XLA Ops:
  0.6 25.6 %copy-start = (bf16[64,256]{1,0:T(8,128)(2,1)S(1)}, bf16[64,256]{1,0:T(8,128)(2,1)}, u32[]{:S(2)}) copy-start(bf16[64,256]{1,0:T(8,128)(2,1)} %factor_c.3) | copy-start | bytes 98308
  5.4 3.4 %collective-permute-start = (f32[4,56,128]{2,1,0:T(8,128)}, f32[4,56,128]{2,1,0:T(8,128)S(1)}, u32[]{:S(2)}, u32[]{:S(2)}) collective-permute-start(f32[4,56,128]{2,1,0:T(8,128)} %get-tuple-element.7), channel_id=1, source_target_pairs={{0,1},{1,0},{2,3},{3,2},{4,5},{5,4},{6,7},{7,6},{8,9},{9,8},{10,11... | collective-permute-start | bytes 344072 | tf_op jit(solution)/shard_map/ppermute | solution.py:360
  23.1 3.2 %collective-permute-start.1 = (f32[4,56,128]{2,1,0:T(8,128)S(1)}, f32[4,56,128]{2,1,0:T(8,128)S(1)}, u32[]{:S(2)}, u32[]{:S(2)}) collective-permute-start(f32[4,56,128]{2,1,0:T(8,128)S(1)} %reduce_sum.27.mine), channel_id=1, source_target_pairs={{0,1},{1,0},{2,3},{3,2},{4,5},{5,4},{6,7},{7,6},{8,9},{9,8},{10,11... | collective-permute-start | bytes 344072 | tf_op jit(solution)/shard_map/ppermute | solution.py:360
  30.0 72.9 %copy-start.1 = (bf16[64,256]{1,0:T(8,128)(2,1)S(1)}, bf16[64,256]{1,0:T(8,128)(2,1)}, u32[]{:S(2)}) copy-start(bf16[64,256]{1,0:T(8,128)(2,1)} %factor_c.3) | copy-start | bytes 98308
  68.5 34.3 %copy-start.2 = (f32[8,16,128]{2,1,0:T(8,128)S(1)}, f32[8,16,128]{2,1,0:T(8,128)}, u32[]{:S(2)}) copy-start(f32[8,16,128]{2,1,0:T(8,128)} %all_to_all.32.sums_in.sums) | copy-start | bytes 196612
  86.5 26.9 %all-to-all-start.4 = ((f32[8,32,256]{2,1,0:T(8,128)}), f32[8,32,256]{2,1,0:T(8,128)S(1)}, u32[]{:S(2)}, u32[]{:S(2)}) async-start(f32[8,32,256]{2,1,0:T(8,128)} %bitcast.3), calls=%async_computation.4 | async-start | bytes 524288 | tf_op jit(solution)/shard_map/all_to_all | solution.py:411

commit v7 on v6

--- a/solution.py
+++ b/solution.py
@@ -24,7 +24,8 @@
 STEPS = 12
 RESIDUAL = 1e-8
 VMEM_BYTES = 24 * 1024 * 1024
-STREAM_BYTES = 115 * 512 * 1024
+FIRST_BYTES = 107 * 512 * 1024
+SECOND_BYTES = 105 * 512 * 1024
 INVERSE_COST = pl.CostEstimate(flops=12_000_000_000, bytes_accessed=1_000_000, transcendentals=0)
 
 
@@ -241,7 +242,7 @@
     give[...] = jnp.where(first, out[1], out[0])
 
 
-def first_solve_kernel(where, mine, other, factor_c, a_hat, slab, work, inverse, raw):
+def first_solve_kernel(where, mine, other, factor_c, a_hat, a_near, slab, work, inverse, raw):
     rank = work.shape[0]
     share = rank // PARTS
     half = PARTS // CORES
@@ -256,6 +257,7 @@
     row, _ = invert_scaled(b_gram * bf16_gram(factor_c[...]), work, inverse)
     rows = dot_nn(m_first * row, inverse[...]) * row
     a_hat[...] = rows
+    a_near[...] = rows
     raw[...] = dot_tn(rows, rows)
     mine = raw[pl.ds(where[0] * share, share), :]
     squares = jnp.sum(rows * rows, axis=0, keepdims=True)
@@ -338,7 +340,7 @@
     )(*operands)
 
 
-def stream(kernel, out_shape, *operands, scalars=(), scratch=()):
+def stream(kernel, out_shape, *operands, vmem, scalars=(), scratch=()):
     return call(
         kernel,
         out_shape,
@@ -350,7 +352,7 @@
             pltpu.SemaphoreType.DMA((len(operands) - 1,)),
             *scratch,
         ],
-        vmem=STREAM_BYTES,
+        vmem=vmem,
         in_specs=[pl.BlockSpec(memory_space=pltpu.SMEM)] * len(scalars)
         + [pl.BlockSpec(memory_space=pl.ANY)] * len(operands),
     )
@@ -383,6 +385,7 @@
         tensor,
         factor_b,
         factor_c,
+        vmem=FIRST_BYTES,
         scalars=[core],
         scratch=[pltpu.VMEM((CORES, *half.shape), jnp.float32)],
     )
@@ -390,9 +393,9 @@
     mine = jnp.sum(gather(pair, "x", PARTS // CORES), axis=0)
     other = swap_cores(mine)
 
-    a_hat, slab = call(
+    a_hat, a_near, slab = call(
         first_solve_kernel,
-        (f32(x_rows, rank), f32(PARTS, 2 * GROUP, LANES)),
+        (f32(x_rows, rank), f32(x_rows, rank), f32(PARTS, 2 * GROUP, LANES)),
         where,
         mine,
         other,
@@ -403,7 +406,13 @@
 
     sums = gather(scatter_sum(slab, "gl"), FAR)
     product = stream(
-        second_mode_kernel, f32(PARTS, y_rows // PARTS + GROUP, rank), tensor, a_hat, sums, factor_c
+        second_mode_kernel,
+        f32(PARTS, y_rows // PARTS + GROUP, rank),
+        tensor,
+        a_near,
+        sums,
+        factor_c,
+        vmem=SECOND_BYTES,
     )
     received = lax.all_to_all(product, "gl", 0, 0)
     halves = jnp.sum(received[:, : y_rows // PARTS], axis=0).reshape(HALVES, y_rows // PARTS // HALVES, rank)

time: 137 us -> 134 us (0.978)
  no operation moved by 1% of the time
where the time goes in v7:
time: 134 us
  blocking collectives  97.6 us (73%)
  Pallas kernels  23.1 us (17%)
  starting transfers between devices  7.25 us (5%)
  waiting for transfers between devices  2.58 us (2%)
  local copies, waits for them, and re-layouts  2.36 us (2%)
    all_to_all x3, blocking collectives, gather(): lax.all_to_all(jnp.broadcast_to(block[None], (size, *block.shape)), axis,...  61.3 us
    pallas_call x5, Pallas kernels, call(): pl.pallas_call(kernel, out_shape=out_shape, scratch_shapes=list(scratch),...  23.1 us
    all_gather x1, blocking collectives, local(): pieces = lax.all_gather(received[:, y_rows // PARTS:, :LANES], GY)  12.8 us
    all_to_all x1, blocking collectives, local(): received = lax.all_to_all(product, 'gl', 0, 0)  11.8 us
    all_to_all x1, blocking collectives, scatter_sum(): return jnp.sum(lax.all_to_all(parts, axis, 0, 0), axis=0)  11.6 us
    ppermute x2, starting transfers between devices, swap_cores(): return lax.ppermute(value, 'core', [(0, 1), (1, 0)])  3.84 us
    all_to_all x1, starting transfers between devices, local(): m_second = lax.all_to_all(repeated, FAR, 0, 0)  3.41 us
  transfers between devices with their start and end apart: 3, of which 2 were waited for; matrix products, arithmetic and copies ran while one was open for 0% of the time, Pallas kernels for 8%

profile of v7, /device:TPU:8, one launch (start us, length us, event | category | flops | bytes accessed | tf_op | source)
XLA Modules:
  0.0 133.8 jit_solution(1915814665995808818)
XLA Ops:
  0.6 0.0 copy-start
  0.6 0.7 copy-done
  1.4 0.0 copy-start.1
  1.4 4.0 %shard_map.50 = (f32[4,56,128]{2,1,0:T(8,128)S(1)}, f32[4,56,128]{2,1,0:T(8,128)S(1)}) custom-call(s32[1]{0:T(128)} %bitcast.1.core, bf16[64,64,512]{2,1,0:T(8,128)(2,1)} %tensor_in.3, bf16[512,256]{1,0:T(8,128)(2,1)} %factor_b_in.1, bf16[64,256]{1,0:T(8,128)(2,1)S(1)} %copy-done), custom_call_target="tpu_custom_call" | custom-call | tf_op jit(solution)/shard_map/pallas_call | solution.py:334
  5.4 1.9 %collective-permute-start = (f32[4,56,128]{2,1,0:T(8,128)S(1)}, f32[4,56,128]{2,1,0:T(8,128)S(1)}, u32[]{:S(2)}, u32[]{:S(2)}) collective-permute-start(f32[4,56,128]{2,1,0:T(8,128)S(1)} %get-tuple-element.8), channel_id=1, source_target_pairs={{0,1},{1,0},{2,3},{3,2},{4,5},{5,4},{6,7},{7,6},{8,9},{9,8},{10,11... | collective-permute-start | bytes 344072 | tf_op jit(solution)/shard_map/ppermute | solution.py:362
  7.4 1.3 collective-permute-done
  8.7 13.2 %all_to_all.30 = f32[4,4,56,128]{3,2,1,0:T(8,128)S(1)} all-to-all(f32[4,4,56,128]{3,2,1,0:T(8,128)S(1)} %broadcast_in_dim.10), channel_id=1, replica_groups=mesh['zh'=4,'zb'=2,'gl'=8,'x'=4,'core'=2] {'x'}, dimensions={0} | all-to-all | bytes 917504 | tf_op jit(solution)/shard_map/all_to_all | solution.py:370
  21.9 1.9 %collective-permute-start.1 = (f32[4,56,128]{2,1,0:T(8,128)S(1)}, f32[4,56,128]{2,1,0:T(8,128)S(1)}, u32[]{:S(2)}, u32[]{:S(2)}) collective-permute-start(f32[4,56,128]{2,1,0:T(8,128)S(1)} %reduce_sum.27.mine), channel_id=1, source_target_pairs={{0,1},{1,0},{2,3},{3,2},{4,5},{5,4},{6,7},{7,6},{8,9},{9,8},{10,11... | collective-permute-start | bytes 344072 | tf_op jit(solution)/shard_map/ppermute | solution.py:362
  23.9 1.3 collective-permute-done.1.other
  25.1 0.0 copy-done.1
  25.2 4.8 %shard_map.51 = (f32[64,256]{1,0:T(8,128)}, f32[64,256]{1,0:T(8,128)S(1)}, f32[8,16,128]{2,1,0:T(8,128)S(1)}) custom-call(s32[1]{0:T(128)} %bitcast.where, f32[4,56,128]{2,1,0:T(8,128)S(1)} %reduce_sum.27.mine, f32[4,56,128]{2,1,0:T(8,128)S(1)} %collective-permute-done.1.other, bf16[64,256]{1,0:T(8,128)(2,1)S(1)} %copy-done.1), custom_call_target="tpu_custom_call" | custom-call | tf_op jit(solution)/shard_map/pallas_call | solution.py:334
  29.9 11.6 %all_to_all.31 = f32[8,16,128]{2,1,0:T(8,128)S(1)} all-to-all(f32[8,16,128]{2,1,0:T(8,128)S(1)} %get-tuple-element.11), channel_id=1, replica_groups=mesh['zh'=4,'zb'=2,'gl'=8,'x'=4,'core'=2] {'gl'}, dimensions={0} | all-to-all | bytes 131072 | tf_op jit(solution)/shard_map/all_to_all | solution.py:366
  41.6 26.7 %all_to_all.32.sums_in.sums = f32[8,16,128]{2,1,0:T(8,128)S(1)} all-to-all(f32[8,16,128]{2,1,0:T(8,128)S(1)} %broadcast_in_dim.11), channel_id=1, replica_groups=mesh['zh'=4,'zb'=2,'gl'=8,'x'=4,'core'=2] {'zh','zb'}, dimensions={0} | all-to-all | bytes 131072 | tf_op jit(solution)/shard_map/all_to_all | solution.py:370
  68.3 3.4 %shard_map.52 = f32[8,72,256]{2,1,0:T(8,128)S(1)} custom-call(bf16[64,64,512]{2,1,0:T(8,128)(2,1)} %tensor_in.3, f32[64,256]{1,0:T(8,128)S(1)} %get-tuple-element.10.a_hat_in, f32[8,16,128]{2,1,0:T(8,128)S(1)} %all_to_all.32.sums_in.sums, bf16[64,256]{1,0:T(8,128)(2,1)S(1)} %copy-done.1), custom_call_target="tpu_custom_call" | custom-call | tf_op jit(solution)/shard_map/pallas_call | solution.py:334
  71.7 11.8 %all_to_all.33 = f32[8,72,256]{2,1,0:T(8,128)S(1)} all-to-all(f32[8,72,256]{2,1,0:T(8,128)S(1)} %shard_map.52), channel_id=1, replica_groups=mesh['zh'=4,'zb'=2,'gl'=8,'x'=4,'core'=2] {'gl'}, dimensions={0} | all-to-all | bytes 1179648 | tf_op jit(solution)/shard_map/all_to_all | solution.py:417
  83.6 0.7 broadcast_in_dim.13
  84.3 3.4 %all-to-all-start.4 = ((f32[8,32,256]{2,1,0:T(8,128)}), f32[8,32,256]{2,1,0:T(8,128)S(1)}, u32[]{:S(2)}, u32[]{:S(2)}) async-start(f32[8,32,256]{2,1,0:T(8,128)} %bitcast.3), calls=%async_computation.4 | async-start | bytes 524288 | tf_op jit(solution)/shard_map/all_to_all | solution.py:420
  87.7 12.8 %all-gather = f32[64,8,128]{2,1,0:T(8,128)S(1)} all-gather(f32[8,8,128]{2,1,0:T(8,128)S(1)} %slice.9), channel_id=2, replica_groups=mesh['zh'=4,'zb'=2,'gl'=8,'x'=4,'core'=2] {'x','core'}, dimensions={0}, use_global_device_ids=true | all-gather | bytes 294912 | tf_op jit(solution)/shard_map/all_gather | solution.py:421
  100.6 10.6 %shard_map.53.inverse = f32[256,256]{1,0:T(8,128)S(1)} custom-call(f32[8,8,8,128]{3,2,1,0:T(8,128)S(1)} %bitcast.6, f32[8,16,128]{2,1,0:T(8,128)S(1)} %all_to_all.32.sums_in.sums, bf16[64,256]{1,0:T(8,128)(2,1)S(1)} %copy-done.1), custom_call_target="tpu_custom_call" | custom-call | flops 12000000000 | bytes 1000000 | tf_op jit(solution)/shard_map/pallas_call | solution.py:334
  111.2 0.0 all-to-all-done.4.m_second
  111.2 0.2 shard_map.54
  111.5 21.4 %all_to_all.34 = f32[16,32,256]{2,1,0:T(8,128)S(1)} all-to-all(f32[16,32,256]{2,1,0:T(8,128)S(1)} %broadcast_in_dim.14), channel_id=1, replica_groups=mesh['zh'=4,'zb'=2,'gl'=8,'x'=4,'core'=2] {'gl','zb'}, dimensions={0} | all-to-all | bytes 1048576 | tf_op jit(solution)/shard_map/all_to_all | solution.py:370
  133.0 0.8 copy.6
  (8 shorter events, 0.2 us)
Async XLA Ops:
  0.6 0.8 copy-start
  1.4 23.8 %copy-start.1 = (bf16[64,256]{1,0:T(8,128)(2,1)S(1)}, bf16[64,256]{1,0:T(8,128)(2,1)}, u32[]{:S(2)}) copy-start(bf16[64,256]{1,0:T(8,128)(2,1)} %factor_c.3) | copy-start | bytes 98308
  5.4 3.2 %collective-permute-start = (f32[4,56,128]{2,1,0:T(8,128)S(1)}, f32[4,56,128]{2,1,0:T(8,128)S(1)}, u32[]{:S(2)}, u32[]{:S(2)}) collective-permute-start(f32[4,56,128]{2,1,0:T(8,128)S(1)} %get-tuple-element.8), channel_id=1, source_target_pairs={{0,1},{1,0},{2,3},{3,2},{4,5},{5,4},{6,7},{7,6},{8,9},{9,8},{10,11... | collective-permute-start | bytes 344072 | tf_op jit(solution)/shard_map/ppermute | solution.py:362
  21.9 3.2 %collective-permute-start.1 = (f32[4,56,128]{2,1,0:T(8,128)S(1)}, f32[4,56,128]{2,1,0:T(8,128)S(1)}, u32[]{:S(2)}, u32[]{:S(2)}) collective-permute-start(f32[4,56,128]{2,1,0:T(8,128)S(1)} %reduce_sum.27.mine), channel_id=1, source_target_pairs={{0,1},{1,0},{2,3},{3,2},{4,5},{5,4},{6,7},{7,6},{8,9},{9,8},{10,11... | collective-permute-start | bytes 344072 | tf_op jit(solution)/shard_map/ppermute | solution.py:362
  84.3 26.9 %all-to-all-start.4 = ((f32[8,32,256]{2,1,0:T(8,128)}), f32[8,32,256]{2,1,0:T(8,128)S(1)}, u32[]{:S(2)}, u32[]{:S(2)}) async-start(f32[8,32,256]{2,1,0:T(8,128)} %bitcast.3), calls=%async_computation.4 | async-start | bytes 524288 | tf_op jit(solution)/shard_map/all_to_all | solution.py:420
